TPU v7x, 32 devices: a whole 2x2x4 slice. The times are simulated.
32 devices in a mesh: rep: 4 (over y, core), fsdp: 8 (over z, x).
Axes of the slice: x: 2, y: 2, z: 4, core: 2. Of those that a mesh axis runs over, the one named last changes fastest.
Arguments:
- tokens: bfloat16 [32768, 8192], P(('rep', 'fsdp')), may hold values from -6 to 6
- cotangent: bfloat16 [32768, 512], P(('rep', 'fsdp')), may hold values from -0.03125 to 0.03125
- old_weight: bfloat16 [8192, 512], P(('rep', 'fsdp')), may hold values from -0.0625 to 0.0625
- old_first: float32 [8192, 512], P(('rep', 'fsdp')), may hold values from -4 to 4
- old_second: float32 [8192, 512], P(('rep', 'fsdp')), may hold values from 0.05 to 2
- old_owner: int32 [32], replicated, may hold values from 0 to 31, each once
- new_owner: int32 [8], replicated, may hold values from 0 to 7, each once
Outputs:
- projected: bfloat16 [32768, 512], P(('rep', 'fsdp'))
- new_weight: bfloat16 [8192, 512], P(('rep', 'fsdp'))
- new_first: float32 [8192, 512], P(('rep', 'fsdp'))
- new_second: float32 [8192, 512], P(('rep', 'fsdp'))
Inputs may be any that keep to these rules, and one draw needn't show every extreme that they name: `old_owner`: a permutation. `new_owner`: a permutation.
All inputs are finite; a program needn't handle non-finite values.
Results may differ from a plain program's by a relative error of at most 0.008.
Values may be sent and summed in bfloat16 or wider, within the bound.
No kernel may reach another device: no remote copies, remote signals or barrier semaphores. Data moves between devices by JAX's collectives and lax.ppermute only.
A program may use at most 192 MiB of HBM per device.

v0:
```python
import functools
import jax
import jax.numpy as jnp
import numpy as np
from jax import lax
from jax.experimental import pallas as pl
from jax.experimental.pallas import tpu as pltpu
from jax.sharding import PartitionSpec as P

beta_one = 0.9
beta_two = 0.95
learn_rate = 0.001
decay_rate = 0.1
epsilon = 1e-08
correction_one = 1.0 - 0.9**10
correction_two = 1.0 - 0.95**10

AXES = ("rep", "fsdp")
MIB = 1024 * 1024
COLUMNS = 2
SUB = 8


def cost(flops, moved):
    return pl.CostEstimate(flops=flops, bytes_accessed=moved, transcendentals=0)


def block_at(new_ref, groups, position):
    shards = new_ref.shape[0]
    return new_ref[lax.rem(position, shards)] * groups + lax.div(position, shards)


def grad_kernel(per_step, adds, outs, row_ref, new_ref, *refs):
    token_refs, turned_ref, refs = refs[:per_step], refs[per_step], refs[per_step + 1 :]
    out_refs = refs[-outs:]

    def write(out_ref):
        for slot, token_ref in enumerate(token_refs):
            block = jnp.dot(turned_ref[...], token_ref[...], preferred_element_type=jnp.float32)
            if adds:
                block = block + refs[0][slot].astype(jnp.float32)
            out_ref[slot] = block.astype(out_ref.dtype)

    if outs == 1:
        write(out_refs[0])
        return
    for part, out_ref in enumerate(out_refs):
        pl.when(pl.program_id(0) == part)(functools.partial(write, out_ref))


def grad_blocks(
    tokens, turned, row, new_owner, first, steps, per_step, addend=None, cut=False, after=()
):
    rows, features = tokens.shape
    width = turned.shape[0]
    blocks = steps * per_step
    groups = lax.axis_size("rep")
    row_block = features // (groups * new_owner.shape[0])
    if row_block % 128:
        chosen = row[first : first + blocks]
        chosen = jnp.take(new_owner, chosen % new_owner.shape[0]) * groups + (
            chosen // new_owner.shape[0]
        )
        whole = jnp.dot(turned, tokens, preferred_element_type=jnp.float32)
        parts = jnp.transpose(whole.reshape(width, features // row_block, row_block), (1, 0, 2))
        parts = jnp.take(parts, chosen, axis=0)
        if addend is not None:
            parts = parts + addend.astype(jnp.float32)
        parts = parts.astype(jnp.bfloat16)
        return list(jnp.split(parts, steps)) if cut else [parts]

    def token_map(slot):
        return lambda i, row_ref, new_ref: (
            0,
            block_at(new_ref, groups, row_ref[first + i * per_step + slot]),
        )

    block = pl.BlockSpec((per_step, width, row_block), lambda i, *_: (i, 0, 0))
    fixed = pl.BlockSpec((per_step, width, row_block), lambda i, *_: (0, 0, 0))
    added = [] if addend is None else [addend]
    outs = steps if cut else 1
    return pl.pallas_call(
        functools.partial(grad_kernel, per_step, len(added), outs),
        grid_spec=pltpu.PrefetchScalarGridSpec(
            num_scalar_prefetch=2,
            grid=(steps,),
            in_specs=[pl.BlockSpec((rows, row_block), token_map(s)) for s in range(per_step)]
            + [pl.BlockSpec((width, rows), lambda i, *_: (0, 0))]
            + [block] * len(added)
            + [pl.BlockSpec(memory_space=pl.ANY)] * len(after),
            out_specs=[fixed if cut else block] * outs,
        ),
        out_shape=[jax.ShapeDtypeStruct((blocks // outs, width, row_block), jnp.bfloat16)] * outs,
        compiler_params=pltpu.CompilerParams(vmem_limit_bytes=46 * MIB),
        cost_estimate=cost(
            2 * rows * width * blocks * row_block,
            2 * blocks * row_block * (rows + width * (1 + len(added))) + 2 * rows * width,
        ),
        name="weight_gradient",
    )(row, new_owner, *([tokens] * per_step), turned, *added, *after)


def pack_kernel(groups, new_ref, first_ref, second_ref, out_ref):
    for slot in range(out_ref.shape[0]):
        block = block_at(new_ref, groups, slot)
        rows = pl.ds(pl.multiple_of(block * SUB, SUB), SUB)
        pair = jnp.concatenate([first_ref[rows, :], second_ref[rows, :]], axis=0)
        out_ref[slot] = pair.astype(out_ref.dtype)


def pack_moments(first, second, new_owner, groups):
    devices = new_owner.shape[0] * groups
    width = first.shape[1]
    return pl.pallas_call(
        functools.partial(pack_kernel, groups),
        in_specs=[
            pl.BlockSpec(memory_space=pltpu.SMEM),
            pl.BlockSpec(memory_space=pltpu.VMEM),
            pl.BlockSpec(memory_space=pltpu.VMEM),
        ],
        out_specs=pl.BlockSpec(memory_space=pltpu.VMEM),
        out_shape=jax.ShapeDtypeStruct((devices, 2 * SUB, width), jnp.bfloat16),
        cost_estimate=cost(0, 12 * first.size),
        name="pack_moments",
    )(new_owner, first, second)


def project_kernel(groups, first, own, count, row_ref, old_ref, new_ref, token_ref, *refs):
    piece_refs, (out_ref, rows_ref, held, logical, sems) = refs[:count], refs[-5:]
    devices, row_block, _ = held.shape

    @pl.when(pl.program_id(0) == 0)
    def _():
        copies = []
        for piece_ref in piece_refs:
            for index in range(piece_ref.shape[0]):
                slot = len(copies)
                target = held.at[old_ref[row_ref[first + slot]]]
                copies.append(pltpu.make_async_copy(piece_ref.at[index], target, sems.at[slot]))
        for copy in copies:
            copy.start()
        for copy in copies:
            copy.wait()

        def place(pair, carry):
            for block in range(0, devices, 2):
                span = pl.ds(block * SUB, 2 * SUB)
                top = held[2 * pair, span, :]
                low = held[2 * pair + 1, span, :]
                for half in range(2):
                    part = slice(half * SUB, (half + 1) * SUB)
                    start = (block + half) * row_block + pair * 2 * SUB
                    logical[pl.ds(pl.multiple_of(start, 2 * SUB), 2 * SUB), :] = jnp.concatenate(
                        [top[part], low[part]], axis=0
                    )
            return carry

        lax.fori_loop(0, devices // 2, place, 0)
        start = block_at(new_ref, groups, row_ref[own]) * row_block
        start = pl.multiple_of(start, row_block)
        rows_ref[...] = logical[pl.ds(start, row_block), :]

    out_ref[...] = jnp.dot(
        token_ref[...], logical[...], preferred_element_type=jnp.float32
    ).astype(out_ref.dtype)


def project(tokens, pieces, row, first, own, old_owner, new_owner, part, parts, before):
    rows, features = tokens.shape
    _, row_block, width = pieces[0].shape
    before = [] if before is None else [before]
    devices = old_owner.shape[0]
    tile = rows // 4
    return pl.pallas_call(
        functools.partial(
            project_kernel, devices // new_owner.shape[0], first, own, len(pieces)
        ),
        grid_spec=pltpu.PrefetchScalarGridSpec(
            num_scalar_prefetch=3,
            grid=(rows // tile,),
            in_specs=[pl.BlockSpec((tile, features), lambda i, *_: (i, 0))]
            + [pl.BlockSpec(memory_space=pl.ANY)] * (len(pieces) + len(before)),
            out_specs=[
                pl.BlockSpec((tile, width), lambda i, *_: (i, part)),
                pl.BlockSpec((row_block, width), lambda i, *_: (0, 0)),
            ],
            scratch_shapes=[
                pltpu.VMEM((devices, row_block, width), jnp.bfloat16),
                pltpu.VMEM((features, width), jnp.bfloat16),
                pltpu.SemaphoreType.DMA((devices,)),
            ],
        ),
        out_shape=[
            jax.ShapeDtypeStruct((rows, parts * width), jnp.bfloat16),
            jax.ShapeDtypeStruct((row_block, width), jnp.bfloat16),
        ],
        input_output_aliases={4 + len(pieces): 0} if before else {},
        compiler_params=pltpu.CompilerParams(vmem_limit_bytes=46 * MIB),
        cost_estimate=cost(
            2 * rows * width * features, 2 * (rows * features + features * width + rows * width)
        ),
        name="project",
    )(row, old_owner, new_owner, tokens, *pieces, *before)


def adam(weight_rows, first_rows, second_rows, gradient):
    first_next = beta_one * first_rows + (1.0 - beta_one) * gradient
    second_next = beta_two * second_rows + (1.0 - beta_two) * gradient * gradient
    step_size = first_next / correction_one / (jnp.sqrt(second_next / correction_two) + epsilon)
    updated = (
        weight_rows.astype(jnp.float32) * (1.0 - learn_rate * decay_rate) - learn_rate * step_size
    ).astype(jnp.bfloat16)
    return updated, first_next, second_next


def adam_kernel(columns, owner_ref, moments_ref, *refs):
    weight_refs, refs = refs[:columns], refs[columns:]
    part_refs, (new_ref, first_ref, second_ref, gradient, inverse_ref) = refs[:-5], refs[-5:]
    for slot in range(moments_ref.shape[0]):
        inverse_ref[owner_ref[slot]] = slot
    total = part_refs[0][0].astype(jnp.float32)
    for part_ref in part_refs[1:]:
        total = total + part_ref[0].astype(jnp.float32)
    gradient[...] = total.T
    for pair in range(moments_ref.shape[0] // 2):
        even = moments_ref[inverse_ref[2 * pair]].astype(jnp.float32)
        odd = moments_ref[inverse_ref[2 * pair + 1]].astype(jnp.float32)
        rows = pl.ds(pair * 2 * SUB, 2 * SUB)
        new_ref[rows, :], first_ref[rows, :], second_ref[rows, :] = adam(
            jnp.concatenate([ref[rows, :] for ref in weight_refs], axis=1),
            jnp.concatenate([even[:SUB], odd[:SUB]], axis=0),
            jnp.concatenate([even[SUB:], odd[SUB:]], axis=0),
            gradient[rows, :],
        )


def adam_rows(parts, moments, weight_rows, owners):
    row_block, columns = weight_rows[0].shape
    width = columns * len(weight_rows)
    whole = pl.BlockSpec((row_block, width), lambda i, *_: (0, 0))
    return pl.pallas_call(
        functools.partial(adam_kernel, len(weight_rows)),
        grid_spec=pltpu.PrefetchScalarGridSpec(
            num_scalar_prefetch=1,
            grid=(1,),
            in_specs=[pl.BlockSpec(moments.shape, lambda i, *_: (0, 0, 0))]
            + [pl.BlockSpec((row_block, columns), lambda i, *_: (0, 0))] * len(weight_rows)
            + [pl.BlockSpec((1, width, row_block), lambda i, *_: (0, 0, 0))] * len(parts),
            out_specs=[whole] * 3,
            scratch_shapes=[
                pltpu.VMEM((row_block, width), jnp.float32),
                pltpu.SMEM((moments.shape[0],), jnp.int32),
            ],
        ),
        out_shape=[
            jax.ShapeDtypeStruct((row_block, width), jnp.bfloat16),
            jax.ShapeDtypeStruct((row_block, width), jnp.float32),
            jax.ShapeDtypeStruct((row_block, width), jnp.float32),
        ],
        compiler_params=pltpu.CompilerParams(vmem_limit_bytes=12 * MIB),
        cost_estimate=cost(20 * row_block * width, 16 * row_block * width),
        name="adam_rows",
    )(owners, moments, *weight_rows, *parts)


class Grid:
    def __init__(self, groups, shards):
        self.shards = shards
        self.cores = 2 if groups % 2 == 0 else 1
        self.minor = 2 if shards % 2 == 0 else 1
        self.outer = groups // self.cores
        self.far = shards // self.minor
        self.swaps = self.cores == 2 and self.minor == self.outer
        self.near, self.side = self.minor, self.outer

    def moved(self, position, core=0, near=0, side=0, far=0):
        group, shard = position // self.shards, position % self.shards
        outer, on = group // self.cores, (group % self.cores + core) % self.cores
        depth, minor = shard // self.minor, shard % self.minor
        swapped = on if self.swaps else 0
        minor = (minor + near + (side - near) * swapped) % self.minor
        outer = (outer + side + (near - side) * swapped) % self.outer
        depth = (depth + far) % self.far
        return (outer * self.cores + on) * self.shards + depth * self.minor + minor

    def send(self, value, **steps):
        devices = self.outer * self.cores * self.shards
        pairs = [(p, self.moved(p, **steps)) for p in range(devices)]
        return lax.ppermute(value, AXES, pairs)


def rounded_sum(terms, start, count):
    total = sum(term[start : start + count].astype(jnp.float32) for term in terms)
    return total.astype(terms[0].dtype)


def sum_chunks(grid):
    half = grid.far // 2
    return [sorted({d, (grid.far - d) % grid.far}) for d in range(half + 1)]


def shard_chunks(grid):
    return [list(range(grid.far))]


def tables(grid, devices):
    sums = [
        dict(core=core, near=near, side=side, far=far)
        for chunk in sum_chunks(grid)
        for core in range(grid.cores)
        for near in [*range(1, grid.near), 0]
        for side in range(grid.side)
        for far in chunk
    ]
    shards = [
        dict(core=-core, near=-near, side=-side, far=-far)
        for chunk in shard_chunks(grid)
        for core in range(grid.cores)
        for near in range(grid.near)
        for side in range(grid.side)
        for far in chunk
    ]
    return np.array(
        [[grid.moved(p, **step) for step in sums + shards] for p in range(devices)], np.int32
    )


def reduce_rows(grid, blocks_of, project_now):
    plan = []
    start = 0
    for number, chunk in enumerate(sum_chunks(grid)):
        plan.insert(0, (number, chunk, start))
        start += len(chunk)
    addends = {}
    if grid.cores > 1:
        for number, chunk, start in plan:
            block = blocks_of(1, number, start, len(chunk), None, False)[0]
            addends[number] = grid.send(block, core=1)
    held = {}
    for number, chunk, start in plan:
        parts = blocks_of(0, number, start, len(chunk), addends.get(number), True)
        held[number] = [parts[-1]]
        for step, part in enumerate(parts[:-1], 1):
            held[number].append(grid.send(part, near=step))
    projection = project_now()
    last = []
    for number, chunk, _ in plan:
        count = len(chunk)
        kept = held[number]
        ends = list(kept)
        for step in range(1, grid.side):
            part = rounded_sum(kept, step * count, count)
            ends.append(grid.send(part, side=step))
        held[number] = ends
    for number, chunk, _ in plan:
        ends = held[number]
        for index, far in enumerate(chunk):
            if not far:
                last.extend(ends)
                continue
            last.append(grid.send(rounded_sum(ends, index, 1), far=far))
    return last, projection


def gather_shards(grid, own):
    arrived = {far: grid.send(own, far=far) for far in range(1, grid.far)}
    arrived[0] = own
    pieces, marks = [], []
    for chunk in shard_chunks(grid):
        base = joined([arrived[far] for far in chunk])
        sides = [grid.send(base, side=step) for step in range(1, grid.side)]
        both = [joined([base] + sides)]
        nears = [grid.send(part, near=step) for step in range(1, grid.near) for part in both]
        marks.append((sides, nears, [arrived[far] for far in chunk]))
        pieces += both + nears
        for core in range(1, grid.cores):
            pieces += [grid.send(part, core=core) for part in both + nears]
    return pieces, marks


def joined(arrays):
    return arrays[0] if len(arrays) == 1 else jnp.concatenate(arrays, axis=0)


def body(tokens, cotangent, old_weight, old_first, old_second, old_owner, new_owner):
    devices = lax.axis_size(AXES)
    groups = lax.axis_size("rep")
    shards = lax.axis_size("fsdp")
    features = tokens.shape[1]
    row_block, width = old_weight.shape
    strip = row_block * width // devices
    grid = Grid(groups, shards)
    me = lax.axis_index(AXES)
    by_tile = row_block == devices * SUB and width % 128 == 0 and devices % 2 == 0

    row = lax.dynamic_index_in_dim(jnp.asarray(tables(grid, devices)), me, 0, keepdims=False)
    per_far = grid.near * grid.side
    own = (grid.near - 1) * grid.side * len(sum_chunks(grid)[0])

    cuts = COLUMNS if by_tile and width % (128 * COLUMNS) == 0 else 1
    gathered = [gather_shards(grid, part[None]) for part in jnp.split(old_weight, cuts, axis=1)]
    marks = [mark for _, part in gathered for mark in part]
    if by_tile:
        packed = pack_moments(old_first, old_second, new_owner, groups)
    else:
        slot_ids = jnp.arange(devices, dtype=jnp.int32)
        placing = jnp.take(new_owner, slot_ids % shards) * groups + slot_ids // shards
        both = jnp.stack([old_first, old_second]).astype(jnp.bfloat16)
        packed = jnp.take(
            jnp.transpose(both.reshape(2, devices, strip), (1, 0, 2)), placing, axis=0
        )
    arrived = lax.all_to_all(packed, AXES, split_axis=0, concat_axis=0, tiled=True)

    turned = cotangent.T

    waits = {}
    if not by_tile:
        waits = {}
    done = []

    def blocks_of(core, chunk, start, count, addend, cut):
        first = (start * grid.cores + core * count) * per_far
        per_step = grid.side * count
        after = [*waits.get((core, chunk), ()), *done[-1:]]
        blocks = grad_blocks(
            tokens, turned, row, new_owner, first, grid.near, per_step, addend, cut, after
        )
        done.append(blocks[0])
        return blocks

    def project_now():
        if not by_tile:
            return ()
        projected, weight_rows = None, []
        for part, (pieces, _) in enumerate(gathered):
            projected, rows = project(
                tokens, pieces, row, devices, own, old_owner, new_owner, part, cuts, projected
            )
            weight_rows.append(rows)
        return projected, weight_rows

    parts, projection = reduce_rows(grid, blocks_of, project_now)
    if by_tile:
        projected, weight_rows = projection
        return (projected, *adam_rows(parts, arrived, weight_rows, old_owner))
    inverse = jnp.zeros((devices,), jnp.int32).at[old_owner].set(slot_ids)
    held = jnp.zeros((devices, devices, strip), jnp.bfloat16)
    held = held.at[jnp.take(old_owner, row[devices:])].set(
        joined(gathered[0][0]).reshape(devices, devices, strip)
    )
    logical = jnp.transpose(held, (1, 0, 2)).reshape(features, width)
    projected = jnp.dot(tokens, logical, preferred_element_type=jnp.float32).astype(jnp.bfloat16)
    own_block = jnp.take(placing, me)
    weight_rows = lax.dynamic_slice_in_dim(logical, own_block * row_block, row_block, 0)
    moved = jnp.transpose(jnp.take(arrived, inverse, axis=0), (1, 0, 2))
    first_rows, second_rows = moved.astype(jnp.float32).reshape(2, row_block, width)
    gradient = sum(part[0].astype(jnp.float32) for part in parts).T
    return (projected, *adam(weight_rows, first_rows, second_rows, gradient))


def solution(mesh):
    placed = P(AXES, None)
    return jax.shard_map(
        body,
        mesh=mesh,
        in_specs=(placed,) * 5 + (P(), P()),
        out_specs=(placed,) * 4,
        check_vma=False,
    )
```

profile of v0, /device:TPU:0, one launch (start us, length us, event | category | flops | bytes accessed | tf_op | source)
XLA Modules:
  0.0 149.6 jit_solution(9550477066737209013)
XLA Ops:
  0.6 0.0 copy-start.7
  0.6 1.5 copy.13
  2.1 0.7 dynamic-slice_bitcast_fusion.row_ref
  2.8 3.3 %weight_gradient.6.refs_5_ = bf16[4,512,256]{2,1,0:T(8,128)(2,1)S(1)} custom-call(s32[64]{0:T(128)S(1)} %dynamic-slice_bitcast_fusion.row_ref, s32[8]{0:T(128)S(1)} %copy-done.7, bf16[1024,8192]{1,0:T(8,128)(2,1)} %refs_1_.11, bf16[1024,8192]{1,0:T(8,128)(2,1)} %refs_1_.11, bf16[512,1024]{1,0:T(8,128)(2,1)S(1)} %bitcast.11), custom_call_target="tpu_custom_call" | custom-call | flops 1073741824 | bytes 4194304 | tf_op jit(solution)/shard_map/weight_gradient/pallas_call | solution.py:82
  6.2 0.0 copy-start.10
  6.2 4.9 %weight_gradient.7.refs_3_ = bf16[8,512,256]{2,1,0:T(8,128)(2,1)S(1)} custom-call(s32[64]{0:T(128)S(1)} %dynamic-slice_bitcast_fusion.row_ref, s32[8]{0:T(128)S(1)} %copy-done.7, bf16[1024,8192]{1,0:T(8,128)(2,1)} %refs_1_.11, bf16[1024,8192]{1,0:T(8,128)(2,1)} %refs_1_.11, bf16[1024,8192]{1,0:T(8,128)(2,1)} %refs_1_.11, bf16[1024,8192]{1,0:T(8,128)(2,1)} %refs_1_.11, ...), custom_call_target="tpu_custom_call" | custom-call | flops 2147483648 | bytes 7340032 | tf_op jit(solution)/shard_map/weight_gradient/pallas_call | solution.py:82
  11.1 0.5 collective-permute-start.18
  11.6 2.6 %collective-permute-start.7 = (bf16[1,256,256]{2,1,0:T(8,128)(2,1)S(1)}, bf16[1,256,256]{2,1,0:T(8,128)(2,1)S(1)}, u32[]{:S(2)}, u32[]{:S(2)}) collective-permute-start(bf16[1,256,256]{2,1,0:T(8,128)(2,1)S(1)} %get-tuple-element.32), channel_id=1, source_target_pairs={{0,2},{1,3},{2,4},{3,5},{4,6},{5,7},{6,0},{7,1},{8,10},{9,11},{10,... | collective-permute-start | bytes 393224 | tf_op jit(solution)/shard_map/ppermute | solution.py:289
  14.3 2.6 %collective-permute-start.8 = (bf16[1,256,256]{2,1,0:T(8,128)(2,1)S(1)}, bf16[1,256,256]{2,1,0:T(8,128)(2,1)S(1)}, u32[]{:S(2)}, u32[]{:S(2)}) collective-permute-start(bf16[1,256,256]{2,1,0:T(8,128)(2,1)S(1)} %get-tuple-element.32), channel_id=1, source_target_pairs={{0,4},{1,5},{2,6},{3,7},{4,0},{5,1},{6,2},{7,3},{8,12},{9,13},{10,... | collective-permute-start | bytes 393224 | tf_op jit(solution)/shard_map/ppermute | solution.py:289
  16.9 1.3 collective-permute-start.9
  18.2 0.7 collective-permute-start
  18.9 1.8 %collective-permute-done.7 = bf16[1,256,256]{2,1,0:T(8,128)(2,1)S(1)} collective-permute-done((bf16[1,256,256]{2,1,0:T(8,128)(2,1)S(1)}, bf16[1,256,256]{2,1,0:T(8,128)(2,1)S(1)}, u32[]{:S(2)}, u32[]{:S(2)}) %collective-permute-start.7) | collective-permute-done | bytes 131104 | tf_op jit(solution)/shard_map/ppermute | solution.py:289
  20.8 0.0 collective-permute-start.14
  20.8 5.6 %collective-permute-done.8 = bf16[1,256,256]{2,1,0:T(8,128)(2,1)S(1)} collective-permute-done((bf16[1,256,256]{2,1,0:T(8,128)(2,1)S(1)}, bf16[1,256,256]{2,1,0:T(8,128)(2,1)S(1)}, u32[]{:S(2)}, u32[]{:S(2)}) %collective-permute-start.8) | collective-permute-done | bytes 131104 | tf_op jit(solution)/shard_map/ppermute | solution.py:289
  26.4 0.9 collective-permute-start.1
  27.3 3.7 %collective-permute-start.2 = (bf16[1,256,256]{2,1,0:T(8,128)(2,1)S(1)}, bf16[1,256,256]{2,1,0:T(8,128)(2,1)S(1)}, u32[]{:S(2)}, u32[]{:S(2)}) collective-permute-start(bf16[1,256,256]{2,1,0:T(8,128)(2,1)S(1)} %get-tuple-element.33), channel_id=1, source_target_pairs={{0,6},{1,7},{2,0},{3,1},{4,2},{5,3},{6,4},{7,5},{8,14},{9,15},{10,... | collective-permute-start | bytes 393224 | tf_op jit(solution)/shard_map/ppermute | solution.py:289
  31.0 0.1 pad_maximum_fusion.1
  31.0 0.0 collective-permute-done
  31.1 1.6 %collective-permute-start.10 = (bf16[4,256,256]{2,1,0:T(8,128)(2,1)S(1)}, bf16[4,256,256]{2,1,0:T(8,128)(2,1)S(1)}, u32[]{:S(2)}, u32[]{:S(2)}) collective-permute-start(bf16[4,256,256]{2,1,0:T(8,128)(2,1)S(1)} %pad_maximum_fusion.1), channel_id=1, source_target_pairs={{0,16},{1,17},{2,18},{3,19},{4,20},{5,21},{6,22},{7,23},{8,9},{9,8... | collective-permute-start | bytes 1572872 | tf_op jit(solution)/shard_map/ppermute | solution.py:289
  32.6 3.3 %weight_gradient.8.refs_4_ = bf16[4,512,256]{2,1,0:T(8,128)(2,1)S(1)} custom-call(s32[64]{0:T(128)S(1)} %dynamic-slice_bitcast_fusion.row_ref, s32[8]{0:T(128)S(1)} %copy-done.7, bf16[1024,8192]{1,0:T(8,128)(2,1)} %refs_1_.11, bf16[1024,8192]{1,0:T(8,128)(2,1)} %refs_1_.11, bf16[512,1024]{1,0:T(8,128)(2,1)S(1)} %bitcast.13, ...), custom_call_target="tpu_custom_call" | custom-call | flops 1073741824 | bytes 4194304 | tf_op jit(solution)/shard_map/weight_gradient/pallas_call | solution.py:82
  36.0 1.4 collective-permute-done.1
  37.4 0.0 collective-permute-start.23
  37.4 2.7 %collective-permute-done.2 = bf16[1,256,256]{2,1,0:T(8,128)(2,1)S(1)} collective-permute-done((bf16[1,256,256]{2,1,0:T(8,128)(2,1)S(1)}, bf16[1,256,256]{2,1,0:T(8,128)(2,1)S(1)}, u32[]{:S(2)}, u32[]{:S(2)}) %collective-permute-start.2) | collective-permute-done | bytes 131104 | tf_op jit(solution)/shard_map/ppermute | solution.py:289
  40.1 0.1 pad_maximum_fusion
  40.2 1.6 %collective-permute-start.3 = (bf16[4,256,256]{2,1,0:T(8,128)(2,1)S(1)}, bf16[4,256,256]{2,1,0:T(8,128)(2,1)S(1)}, u32[]{:S(2)}, u32[]{:S(2)}) collective-permute-start(bf16[4,256,256]{2,1,0:T(8,128)(2,1)S(1)} %pad_maximum_fusion), channel_id=1, source_target_pairs={{0,16},{1,17},{2,18},{3,19},{4,20},{5,21},{6,22},{7,23},{8,9},{9,8... | collective-permute-start | bytes 1572872 | tf_op jit(solution)/shard_map/ppermute | solution.py:289
  41.8 0.0 collective-permute-done.10
  41.9 1.6 %collective-permute-start.11 = (bf16[8,256,256]{2,1,0:T(8,128)(2,1)S(1)}, bf16[8,256,256]{2,1,0:T(8,128)(2,1)}, u32[]{:S(2)}, u32[]{:S(2)}) collective-permute-start(bf16[8,256,256]{2,1,0:T(8,128)(2,1)S(1)} %constant_dynamic-update-slice_fusion.5.refs_0_), channel_id=1, source_target_pairs={{0,1},{1,0},{2,3},{3,2},{4,5},{5,4},{6,7},{7,6},{8,24},{9,25},{10,... | collective-permute-start | bytes 3145736 | tf_op jit(solution)/shard_map/ppermute | solution.py:289
  43.5 3.4 %weight_gradient.9 = (bf16[2,512,256]{2,1,0:T(8,128)(2,1)S(1)}, bf16[2,512,256]{2,1,0:T(8,128)(2,1)S(1)}) custom-call(s32[64]{0:T(128)S(1)} %dynamic-slice_bitcast_fusion.row_ref, s32[8]{0:T(128)S(1)} %copy-done.7, bf16[1024,8192]{1,0:T(8,128)(2,1)} %refs_1_.11, bf16[1024,8192]{1,0:T(8,128)(2,1)} %refs_1_.11, bf16[512,1024]{1,0:T(8,128)(2,1)S(1)} %bitcast.14, ...), custom_call_target="tpu_custom_call" | custom-call | flops 1073741824 | bytes 5242880 | tf_op jit(solution)/shard_map/weight_gradient/pallas_call | solution.py:82
  46.9 0.6 collective-permute-start.15
  47.5 7.2 %collective-permute-done.3 = bf16[4,256,256]{2,1,0:T(8,128)(2,1)S(1)} collective-permute-done((bf16[4,256,256]{2,1,0:T(8,128)(2,1)S(1)}, bf16[4,256,256]{2,1,0:T(8,128)(2,1)S(1)}, u32[]{:S(2)}, u32[]{:S(2)}) %collective-permute-start.3) | collective-permute-done | bytes 524320 | tf_op jit(solution)/shard_map/ppermute | solution.py:289
  54.7 1.9 %collective-permute-start.4 = (bf16[8,256,256]{2,1,0:T(8,128)(2,1)S(1)}, bf16[8,256,256]{2,1,0:T(8,128)(2,1)}, u32[]{:S(2)}, u32[]{:S(2)}) collective-permute-start(bf16[8,256,256]{2,1,0:T(8,128)(2,1)S(1)} %constant_dynamic-update-slice_fusion.refs_0_), channel_id=1, source_target_pairs={{0,1},{1,0},{2,3},{3,2},{4,5},{5,4},{6,7},{7,6},{8,24},{9,25},{10,... | collective-permute-start | bytes 3145736 | tf_op jit(solution)/shard_map/ppermute | solution.py:289
  56.6 0.0 collective-permute-done.18.refs_5_
  56.6 5.8 %weight_gradient.10 = (bf16[4,512,256]{2,1,0:T(8,128)(2,1)}, bf16[4,512,256]{2,1,0:T(8,128)(2,1)S(1)}) custom-call(s32[64]{0:T(128)S(1)} %dynamic-slice_bitcast_fusion.row_ref, s32[8]{0:T(128)S(1)} %copy-done.7, bf16[1024,8192]{1,0:T(8,128)(2,1)} %refs_1_.11, bf16[1024,8192]{1,0:T(8,128)(2,1)} %refs_1_.11, bf16[1024,8192]{1,0:T(8,128)(2,1)} %refs_1_.11, ...), custom_call_target="tpu_custom_call" | custom-call | flops 2147483648 | bytes 9437184 | tf_op jit(solution)/shard_map/weight_gradient/pallas_call | solution.py:82
  62.4 1.0 copy-done.2
  63.3 0.2 collective-permute-start.19
  63.6 1.8 %collective-permute-done.15 = bf16[2,512,256]{2,1,0:T(8,128)(2,1)S(1)} collective-permute-done((bf16[2,512,256]{2,1,0:T(8,128)(2,1)S(1)}, bf16[2,512,256]{2,1,0:T(8,128)(2,1)S(1)}, u32[]{:S(2)}, u32[]{:S(2)}) %collective-permute-start.15) | collective-permute-done | bytes 524320 | tf_op jit(solution)/shard_map/ppermute | solution.py:289
  65.4 1.1 collective-permute-start.12
  66.5 0.0 collective-permute-done.11.refs_1_
  66.5 0.1 collective-permute-start.13
  66.6 0.1 add_convert_fusion.5
  66.7 1.6 %collective-permute-start.16 = (bf16[1,512,256]{2,1,0:T(8,128)(2,1)S(1)}, bf16[1,512,256]{2,1,0:T(8,128)(2,1)S(1)}, u32[]{:S(2)}, u32[]{:S(2)}) collective-permute-start(bf16[1,512,256]{2,1,0:T(8,128)(2,1)S(1)} %add_convert_fusion.5), channel_id=1, source_target_pairs={{0,16},{1,17},{2,18},{3,19},{4,20},{5,21},{6,22},{7,23},{8,9},{9,8... | collective-permute-start | bytes 786440 | tf_op jit(solution)/shard_map/ppermute | solution.py:289
  68.3 4.1 %weight_gradient.11 = (bf16[2,512,256]{2,1,0:T(8,128)(2,1)}, bf16[2,512,256]{2,1,0:T(8,128)(2,1)S(1)}) custom-call(s32[64]{0:T(128)S(1)} %dynamic-slice_bitcast_fusion.row_ref, s32[8]{0:T(128)S(1)} %copy-done.7, bf16[1024,8192]{1,0:T(8,128)(2,1)} %refs_1_.11, bf16[1024,8192]{1,0:T(8,128)(2,1)} %refs_1_.11, bf16[512,1024]{1,0:T(8,128)(2,1)S(1)} %bitcast.16, ...), custom_call_target="tpu_custom_call" | custom-call | flops 1073741824 | bytes 5242880 | tf_op jit(solution)/shard_map/weight_gradient/pallas_call | solution.py:82
  72.4 0.8 copy-done
  73.2 2.7 %collective-permute-done.16 = bf16[1,512,256]{2,1,0:T(8,128)(2,1)S(1)} collective-permute-done((bf16[1,512,256]{2,1,0:T(8,128)(2,1)S(1)}, bf16[1,512,256]{2,1,0:T(8,128)(2,1)S(1)}, u32[]{:S(2)}, u32[]{:S(2)}) %collective-permute-start.16) | collective-permute-done | bytes 262176 | tf_op jit(solution)/shard_map/ppermute | solution.py:289
  76.0 1.0 collective-permute-start.24
  77.0 2.1 %pack_moments.1 = bf16[32,16,512]{2,1,0:T(8,128)(2,1)} custom-call(s32[8]{0:T(128)} %new_ref.17, f32[256,512]{1,0:T(8,128)} %first_ref.1, f32[256,512]{1,0:T(8,128)} %second_ref.1), custom_call_target="tpu_custom_call" | custom-call | bytes 1572864 | tf_op jit(solution)/shard_map/pack_moments/pallas_call | solution.py:114
  79.1 5.7 %all-to-all-start = ((bf16[32,16,512]{2,1,0:T(8,128)(2,1)}), bf16[32,16,512]{2,1,0:T(8,128)(2,1)S(1)}, u32[]{:S(2)}, u32[]{:S(2)}) async-start(bf16[32,16,512]{2,1,0:T(8,128)(2,1)} %pack_moments.1), calls=%async_computation | async-start | bytes 1048576 | tf_op jit(solution)/shard_map/all_to_all | solution.py:412
  84.7 1.9 %add_convert_fusion.4 = bf16[1,512,256]{2,1,0:T(8,128)(2,1)} fusion(bf16[1,512,256]{2,1,0:T(8,128)(2,1)S(1)} %collective-permute-done.16, bf16[2,512,256]{2,1,0:T(8,128)(2,1)} %copy-done.11, bf16[2,512,256]{2,1,0:T(8,128)(2,1)} %copy-done.4), kind=kLoop, calls=%fused_computation.6 | loop fusion | flops 786432 | bytes 1048576 | tf_op jit(solution)/shard_map/convert_element_type | solution.py:294
  86.6 0.3 collective-permute-start.5
  86.8 8.3 %collective-permute-done.19 = bf16[4,512,256]{2,1,0:T(8,128)(2,1)} collective-permute-done((bf16[4,512,256]{2,1,0:T(8,128)(2,1)}, bf16[4,512,256]{2,1,0:T(8,128)(2,1)}, u32[]{:S(2)}, u32[]{:S(2)}) %collective-permute-start.19) | collective-permute-done | bytes 1048608 | tf_op jit(solution)/shard_map/ppermute | solution.py:289
  95.2 0.9 collective-permute-start.6
  96.0 1.3 add_convert_fusion
  97.3 4.0 %collective-permute-done.24.refs_6_ = bf16[2,512,256]{2,1,0:T(8,128)(2,1)} collective-permute-done((bf16[2,512,256]{2,1,0:T(8,128)(2,1)}, bf16[2,512,256]{2,1,0:T(8,128)(2,1)}, u32[]{:S(2)}, u32[]{:S(2)}) %collective-permute-start.24) | collective-permute-done | bytes 524320 | tf_op jit(solution)/shard_map/ppermute | solution.py:289
  101.3 1.5 %collective-permute-start.20 = (bf16[2,512,256]{2,1,0:T(8,128)(2,1)S(1)}, bf16[2,512,256]{2,1,0:T(8,128)(2,1)S(1)}, u32[]{:S(2)}, u32[]{:S(2)}) collective-permute-start(bf16[2,512,256]{2,1,0:T(8,128)(2,1)S(1)} %add_convert_fusion), channel_id=1, source_target_pairs={{0,16},{1,17},{2,18},{3,19},{4,20},{5,21},{6,22},{7,23},{8,9},{9,8... | collective-permute-start | bytes 1572872 | tf_op jit(solution)/shard_map/ppermute | solution.py:289
  102.8 1.7 %add_convert_fusion.1 = bf16[1,512,256]{2,1,0:T(8,128)(2,1)} fusion(bf16[2,512,256]{2,1,0:T(8,128)(2,1)} %collective-permute-done.24.refs_6_, bf16[2,512,256]{2,1,0:T(8,128)(2,1)S(1)} %copy-done.1), kind=kLoop, calls=%fused_computation.3 | loop fusion | flops 524288 | bytes 786432 | tf_op jit(solution)/shard_map/convert_element_type | solution.py:294
  104.6 3.1 %collective-permute-start.17 = (bf16[1,512,256]{2,1,0:T(8,128)(2,1)}, bf16[1,512,256]{2,1,0:T(8,128)(2,1)S(1)}, u32[]{:S(2)}, u32[]{:S(2)}) collective-permute-start(bf16[1,512,256]{2,1,0:T(8,128)(2,1)} %add_convert_fusion.4), channel_id=1, source_target_pairs={{0,4},{1,5},{2,6},{3,7},{4,0},{5,1},{6,2},{7,3},{8,12},{9,13},{10,... | collective-permute-start | bytes 786440 | tf_op jit(solution)/shard_map/ppermute | solution.py:289
  107.7 1.2 collective-permute-start.25
  108.9 14.2 %project.2 = (bf16[1024,512]{1,0:T(8,128)(2,1)}, bf16[256,256]{1,0:T(8,128)(2,1)S(1)}) custom-call(s32[64]{0:T(128)S(1)} %dynamic-slice_bitcast_fusion.row_ref, s32[32]{0:T(128)S(1)} %copy-done.9, s32[8]{0:T(128)S(1)} %copy-done.8, bf16[1024,8192]{1,0:T(8,128)(2,1)} %refs_1_.11, bf16[8,256,256]{2,1,0:T(8,128)(2,1)S(1)} %constant_dynamic-update-slice_fusion.5.refs_0_, ...), custom_call_target="tpu_custom_call" | custom-call | flops 4294967296 | bytes 21495808 | tf_op jit(solution)/shard_map/project/pallas_call | solution.py:174
  123.0 2.1 %add_convert_fusion.2 = (bf16[1,512,256]{2,1,0:T(8,128)(2,1)}, bf16[1,512,256]{2,1,0:T(8,128)(2,1)}) fusion(bf16[2,512,256]{2,1,0:T(8,128)(2,1)S(1)} %collective-permute-done.20, bf16[4,512,256]{2,1,0:T(8,128)(2,1)} %collective-permute-done.19, bf16[4,512,256]{2,1,0:T(8,128)(2,1)S(1)} %copy-done.3), kind=kLoop, calls=%fused_computation.4 | loop fusion | flops 1572864 | bytes 2097152 | tf_op jit(solution)/shard_map/convert_element_type | solution.py:294
  125.1 3.8 %collective-permute-start.22 = (bf16[1,512,256]{2,1,0:T(8,128)(2,1)}, bf16[1,512,256]{2,1,0:T(8,128)(2,1)}, u32[]{:S(2)}, u32[]{:S(2)}) collective-permute-start(bf16[1,512,256]{2,1,0:T(8,128)(2,1)} %get-tuple-element.30), channel_id=1, source_target_pairs={{0,6},{1,7},{2,0},{3,1},{4,2},{5,3},{6,4},{7,5},{8,14},{9,15},{10,... | collective-permute-start | bytes 786440 | tf_op jit(solution)/shard_map/ppermute | solution.py:289
  129.0 15.6 %project.3 = (bf16[1024,512]{1,0:T(8,128)(2,1)}, bf16[256,256]{1,0:T(8,128)(2,1)S(1)}) custom-call(s32[64]{0:T(128)S(1)} %dynamic-slice_bitcast_fusion.row_ref, s32[32]{0:T(128)S(1)} %copy-done.9, s32[8]{0:T(128)S(1)} %copy-done.8, bf16[1024,8192]{1,0:T(8,128)(2,1)} %refs_1_.11, ...), custom_call_target="tpu_custom_call", output_to_operand_aliasing={{0}: (8, {})} | custom-call | flops 4294967296 | bytes 21495808 | tf_op jit(solution)/shard_map/project/pallas_call | solution.py:174
  144.6 0.6 copy-done.5
  145.3 0.9 copy-done.6
  146.2 3.4 %adam_rows.1 = (bf16[256,512]{1,0:T(8,128)(2,1)}, f32[256,512]{1,0:T(8,128)}, f32[256,512]{1,0:T(8,128)}) custom-call(s32[32]{0:T(128)S(1)} %copy-done.9, bf16[32,16,512]{2,1,0:T(8,128)(2,1)S(1)} %all-to-all-done.moments_ref, bf16[256,256]{1,0:T(8,128)(2,1)S(1)} %get-tuple-element.19.refs_0_, bf16[256,256]{1,0:T(8,128)(2,1)S(1)} %copy-done.6, ...), custom_call_target="tpu_custom_call" | custom-call | flops 2621440 | bytes 2097152 | tf_op jit(solution)/shard_map/adam_rows/pallas_call | solution.py:241
  (43 shorter events, 0.2 us)
Async XLA Ops:
  0.6 2.2 %copy-start.7 = (s32[8]{0:T(128)S(1)}, s32[8]{0:T(128)}, u32[]{:S(2)}) copy-start(s32[8]{0:T(128)} %new_ref.17) | copy-start | bytes 100
  6.2 5.4 %copy-start.10 = (bf16[256,512]{1,0:T(8,128)(2,1)S(1)}, bf16[256,512]{1,0:T(8,128)(2,1)}, u32[]{:S(2)}) copy-start(bf16[256,512]{1,0:T(8,128)(2,1)} %param.10) | copy-start | bytes 786436
  11.1 45.5 %collective-permute-start.18 = (bf16[8,512,256]{2,1,0:T(8,128)(2,1)S(1)}, bf16[8,512,256]{2,1,0:T(8,128)(2,1)S(1)}, u32[]{:S(2)}, u32[]{:S(2)}) collective-permute-start(bf16[8,512,256]{2,1,0:T(8,128)(2,1)S(1)} %weight_gradient.7.refs_3_), channel_id=1, source_target_pairs={{0,8},{1,9},{2,10},{3,11},{4,12},{5,13},{6,14},{7,15},{8,0},{9,1},... | collective-permute-start | bytes 6291464 | tf_op jit(solution)/shard_map/ppermute | solution.py:289
  11.6 9.1 %collective-permute-start.7 = (bf16[1,256,256]{2,1,0:T(8,128)(2,1)S(1)}, bf16[1,256,256]{2,1,0:T(8,128)(2,1)S(1)}, u32[]{:S(2)}, u32[]{:S(2)}) collective-permute-start(bf16[1,256,256]{2,1,0:T(8,128)(2,1)S(1)} %get-tuple-element.32), channel_id=1, source_target_pairs={{0,2},{1,3},{2,4},{3,5},{4,6},{5,7},{6,0},{7,1},{8,10},{9,11},{10,... | collective-permute-start | bytes 393224 | tf_op jit(solution)/shard_map/ppermute | solution.py:289
  14.3 12.1 %collective-permute-start.8 = (bf16[1,256,256]{2,1,0:T(8,128)(2,1)S(1)}, bf16[1,256,256]{2,1,0:T(8,128)(2,1)S(1)}, u32[]{:S(2)}, u32[]{:S(2)}) collective-permute-start(bf16[1,256,256]{2,1,0:T(8,128)(2,1)S(1)} %get-tuple-element.32), channel_id=1, source_target_pairs={{0,4},{1,5},{2,6},{3,7},{4,0},{5,1},{6,2},{7,3},{8,12},{9,13},{10,... | collective-permute-start | bytes 393224 | tf_op jit(solution)/shard_map/ppermute | solution.py:289
  16.9 10.4 %collective-permute-start.9 = (bf16[1,256,256]{2,1,0:T(8,128)(2,1)S(1)}, bf16[1,256,256]{2,1,0:T(8,128)(2,1)S(1)}, u32[]{:S(2)}, u32[]{:S(2)}) collective-permute-start(bf16[1,256,256]{2,1,0:T(8,128)(2,1)S(1)} %get-tuple-element.32), channel_id=1, source_target_pairs={{0,6},{1,7},{2,0},{3,1},{4,2},{5,3},{6,4},{7,5},{8,14},{9,15},{10,... | collective-permute-start | bytes 393224 | tf_op jit(solution)/shard_map/ppermute | solution.py:289
  18.2 12.8 %collective-permute-start = (bf16[1,256,256]{2,1,0:T(8,128)(2,1)S(1)}, bf16[1,256,256]{2,1,0:T(8,128)(2,1)S(1)}, u32[]{:S(2)}, u32[]{:S(2)}) collective-permute-start(bf16[1,256,256]{2,1,0:T(8,128)(2,1)S(1)} %get-tuple-element.33), channel_id=1, source_target_pairs={{0,2},{1,3},{2,4},{3,5},{4,6},{5,7},{6,0},{7,1},{8,10},{9,11},{10,... | collective-permute-start | bytes 393224 | tf_op jit(solution)/shard_map/ppermute | solution.py:289
  20.8 22.7 %collective-permute-start.14 = (bf16[4,512,256]{2,1,0:T(8,128)(2,1)S(1)}, bf16[4,512,256]{2,1,0:T(8,128)(2,1)S(1)}, u32[]{:S(2)}, u32[]{:S(2)}) collective-permute-start(bf16[4,512,256]{2,1,0:T(8,128)(2,1)S(1)} %weight_gradient.6.refs_5_), channel_id=1, source_target_pairs={{0,8},{1,9},{2,10},{3,11},{4,12},{5,13},{6,14},{7,15},{8,0},{9,1},... | collective-permute-start | bytes 3145736 | tf_op jit(solution)/shard_map/ppermute | solution.py:289
  26.4 11.1 %collective-permute-start.1 = (bf16[1,256,256]{2,1,0:T(8,128)(2,1)S(1)}, bf16[1,256,256]{2,1,0:T(8,128)(2,1)S(1)}, u32[]{:S(2)}, u32[]{:S(2)}) collective-permute-start(bf16[1,256,256]{2,1,0:T(8,128)(2,1)S(1)} %get-tuple-element.33), channel_id=1, source_target_pairs={{0,4},{1,5},{2,6},{3,7},{4,0},{5,1},{6,2},{7,3},{8,12},{9,13},{10,... | collective-permute-start | bytes 393224 | tf_op jit(solution)/shard_map/ppermute | solution.py:289
  27.3 12.9 %collective-permute-start.2 = (bf16[1,256,256]{2,1,0:T(8,128)(2,1)S(1)}, bf16[1,256,256]{2,1,0:T(8,128)(2,1)S(1)}, u32[]{:S(2)}, u32[]{:S(2)}) collective-permute-start(bf16[1,256,256]{2,1,0:T(8,128)(2,1)S(1)} %get-tuple-element.33), channel_id=1, source_target_pairs={{0,6},{1,7},{2,0},{3,1},{4,2},{5,3},{6,4},{7,5},{8,14},{9,15},{10,... | collective-permute-start | bytes 393224 | tf_op jit(solution)/shard_map/ppermute | solution.py:289
  31.1 10.8 %collective-permute-start.10 = (bf16[4,256,256]{2,1,0:T(8,128)(2,1)S(1)}, bf16[4,256,256]{2,1,0:T(8,128)(2,1)S(1)}, u32[]{:S(2)}, u32[]{:S(2)}) collective-permute-start(bf16[4,256,256]{2,1,0:T(8,128)(2,1)S(1)} %pad_maximum_fusion.1), channel_id=1, source_target_pairs={{0,16},{1,17},{2,18},{3,19},{4,20},{5,21},{6,22},{7,23},{8,9},{9,8... | collective-permute-start | bytes 1572872 | tf_op jit(solution)/shard_map/ppermute | solution.py:289
  37.4 29.2 %collective-permute-start.23 = (bf16[4,512,256]{2,1,0:T(8,128)(2,1)S(1)}, bf16[4,512,256]{2,1,0:T(8,128)(2,1)S(1)}, u32[]{:S(2)}, u32[]{:S(2)}) collective-permute-start(bf16[4,512,256]{2,1,0:T(8,128)(2,1)S(1)} %weight_gradient.8.refs_4_), channel_id=1, source_target_pairs={{0,8},{1,9},{2,10},{3,11},{4,12},{5,13},{6,14},{7,15},{8,0},{9,1},... | collective-permute-start | bytes 3145736 | tf_op jit(solution)/shard_map/ppermute | solution.py:289
  40.2 14.5 %collective-permute-start.3 = (bf16[4,256,256]{2,1,0:T(8,128)(2,1)S(1)}, bf16[4,256,256]{2,1,0:T(8,128)(2,1)S(1)}, u32[]{:S(2)}, u32[]{:S(2)}) collective-permute-start(bf16[4,256,256]{2,1,0:T(8,128)(2,1)S(1)} %pad_maximum_fusion), channel_id=1, source_target_pairs={{0,16},{1,17},{2,18},{3,19},{4,20},{5,21},{6,22},{7,23},{8,9},{9,8... | collective-permute-start | bytes 1572872 | tf_op jit(solution)/shard_map/ppermute | solution.py:289
  41.9 24.6 %collective-permute-start.11 = (bf16[8,256,256]{2,1,0:T(8,128)(2,1)S(1)}, bf16[8,256,256]{2,1,0:T(8,128)(2,1)}, u32[]{:S(2)}, u32[]{:S(2)}) collective-permute-start(bf16[8,256,256]{2,1,0:T(8,128)(2,1)S(1)} %constant_dynamic-update-slice_fusion.5.refs_0_), channel_id=1, source_target_pairs={{0,1},{1,0},{2,3},{3,2},{4,5},{5,4},{6,7},{7,6},{8,24},{9,25},{10,... | collective-permute-start | bytes 3145736 | tf_op jit(solution)/shard_map/ppermute | solution.py:289
  46.9 19.7 %copy-start.4 = (bf16[2,512,256]{2,1,0:T(8,128)(2,1)}, bf16[2,512,256]{2,1,0:T(8,128)(2,1)S(1)}, u32[]{:S(2)}) copy-start(bf16[2,512,256]{2,1,0:T(8,128)(2,1)S(1)} %get-tuple-element.21) | copy-start | bytes 1572868
  46.9 18.5 %collective-permute-start.15 = (bf16[2,512,256]{2,1,0:T(8,128)(2,1)S(1)}, bf16[2,512,256]{2,1,0:T(8,128)(2,1)S(1)}, u32[]{:S(2)}, u32[]{:S(2)}) collective-permute-start(bf16[2,512,256]{2,1,0:T(8,128)(2,1)S(1)} %get-tuple-element.22.refs_6_), channel_id=1, source_target_pairs={{0,1},{1,0},{2,3},{3,2},{4,5},{5,4},{6,7},{7,6},{8,24},{9,25},{10,... | collective-permute-start | bytes 1572872 | tf_op jit(solution)/shard_map/ppermute | solution.py:289
  54.7 31.9 %collective-permute-start.4 = (bf16[8,256,256]{2,1,0:T(8,128)(2,1)S(1)}, bf16[8,256,256]{2,1,0:T(8,128)(2,1)}, u32[]{:S(2)}, u32[]{:S(2)}) collective-permute-start(bf16[8,256,256]{2,1,0:T(8,128)(2,1)S(1)} %constant_dynamic-update-slice_fusion.refs_0_), channel_id=1, source_target_pairs={{0,1},{1,0},{2,3},{3,2},{4,5},{5,4},{6,7},{7,6},{8,24},{9,25},{10,... | collective-permute-start | bytes 3145736 | tf_op jit(solution)/shard_map/ppermute | solution.py:289
  62.4 1.0 copy-start.2
  63.3 31.8 %collective-permute-start.19 = (bf16[4,512,256]{2,1,0:T(8,128)(2,1)}, bf16[4,512,256]{2,1,0:T(8,128)(2,1)}, u32[]{:S(2)}, u32[]{:S(2)}) collective-permute-start(bf16[4,512,256]{2,1,0:T(8,128)(2,1)} %get-tuple-element.24.refs_4_), channel_id=1, source_target_pairs={{0,1},{1,0},{2,3},{3,2},{4,5},{5,4},{6,7},{7,6},{8,24},{9,25},{10,... | collective-permute-start | bytes 3145736 | tf_op jit(solution)/shard_map/ppermute | solution.py:289
  65.4 7.0 %copy-start.11 = (bf16[2,512,256]{2,1,0:T(8,128)(2,1)}, bf16[2,512,256]{2,1,0:T(8,128)(2,1)S(1)}, u32[]{:S(2)}) copy-start(bf16[2,512,256]{2,1,0:T(8,128)(2,1)S(1)} %collective-permute-done.15) | copy-start | bytes 1572868
  65.4 39.2 %collective-permute-start.12 = (bf16[8,256,256]{2,1,0:T(8,128)(2,1)S(1)}, bf16[8,256,256]{2,1,0:T(8,128)(2,1)}, u32[]{:S(2)}, u32[]{:S(2)}) collective-permute-start(bf16[8,256,256]{2,1,0:T(8,128)(2,1)S(1)} %constant_dynamic-update-slice_fusion.5.refs_0_), channel_id=1, source_target_pairs={{0,8},{1,9},{2,10},{3,11},{4,12},{5,13},{6,14},{7,15},{8,0},{9,1},... | collective-permute-start | bytes 3145736 | tf_op jit(solution)/shard_map/ppermute | solution.py:289
  66.5 41.1 %collective-permute-start.13 = (bf16[8,256,256]{2,1,0:T(8,128)(2,1)}, bf16[8,256,256]{2,1,0:T(8,128)(2,1)}, u32[]{:S(2)}, u32[]{:S(2)}) collective-permute-start(bf16[8,256,256]{2,1,0:T(8,128)(2,1)} %collective-permute-done.11.refs_1_), channel_id=1, source_target_pairs={{0,8},{1,9},{2,10},{3,11},{4,12},{5,13},{6,14},{7,15},{8,0},{9,1},... | collective-permute-start | bytes 3145736 | tf_op jit(solution)/shard_map/ppermute | solution.py:289
  66.7 9.3 %collective-permute-start.16 = (bf16[1,512,256]{2,1,0:T(8,128)(2,1)S(1)}, bf16[1,512,256]{2,1,0:T(8,128)(2,1)S(1)}, u32[]{:S(2)}, u32[]{:S(2)}) collective-permute-start(bf16[1,512,256]{2,1,0:T(8,128)(2,1)S(1)} %add_convert_fusion.5), channel_id=1, source_target_pairs={{0,16},{1,17},{2,18},{3,19},{4,20},{5,21},{6,22},{7,23},{8,9},{9,8... | collective-permute-start | bytes 786440 | tf_op jit(solution)/shard_map/ppermute | solution.py:289
  72.4 0.8 copy-start
  76.0 25.3 %collective-permute-start.24 = (bf16[2,512,256]{2,1,0:T(8,128)(2,1)}, bf16[2,512,256]{2,1,0:T(8,128)(2,1)}, u32[]{:S(2)}, u32[]{:S(2)}) collective-permute-start(bf16[2,512,256]{2,1,0:T(8,128)(2,1)} %get-tuple-element.26), channel_id=1, source_target_pairs={{0,1},{1,0},{2,3},{3,2},{4,5},{5,4},{6,7},{7,6},{8,24},{9,25},{10,... | collective-permute-start | bytes 1572872 | tf_op jit(solution)/shard_map/ppermute | solution.py:289
  79.0 23.8 %copy-start.1 = (bf16[2,512,256]{2,1,0:T(8,128)(2,1)S(1)}, bf16[2,512,256]{2,1,0:T(8,128)(2,1)}, u32[]{:S(2)}) copy-start(bf16[2,512,256]{2,1,0:T(8,128)(2,1)} %copy-done) | copy-start | bytes 1572868
  79.0 29.8 %copy-start.8 = (s32[8]{0:T(128)S(1)}, s32[8]{0:T(128)}, u32[]{:S(2)}) copy-start(s32[8]{0:T(128)} %new_ref.17) | copy-start | bytes 100
  79.1 29.8 %copy-start.9 = (s32[32]{0:T(128)S(1)}, s32[32]{0:T(128)}, u32[]{:S(2)}) copy-start(s32[32]{0:T(128)} %owner_ref.1) | copy-start | bytes 388
  79.1 66.2 %all-to-all-start = ((bf16[32,16,512]{2,1,0:T(8,128)(2,1)}), bf16[32,16,512]{2,1,0:T(8,128)(2,1)S(1)}, u32[]{:S(2)}, u32[]{:S(2)}) async-start(bf16[32,16,512]{2,1,0:T(8,128)(2,1)} %pack_moments.1), calls=%async_computation | async-start | bytes 1048576 | tf_op jit(solution)/shard_map/all_to_all | solution.py:412
  86.6 38.6 %collective-permute-start.5 = (bf16[8,256,256]{2,1,0:T(8,128)(2,1)S(1)}, bf16[8,256,256]{2,1,0:T(8,128)(2,1)S(1)}, u32[]{:S(2)}, u32[]{:S(2)}) collective-permute-start(bf16[8,256,256]{2,1,0:T(8,128)(2,1)S(1)} %constant_dynamic-update-slice_fusion.refs_0_), channel_id=1, source_target_pairs={{0,8},{1,9},{2,10},{3,11},{4,12},{5,13},{6,14},{7,15},{8,0},{9,1},... | collective-permute-start | bytes 3145736 | tf_op jit(solution)/shard_map/ppermute | solution.py:289
  95.2 33.8 %collective-permute-start.6 = (bf16[8,256,256]{2,1,0:T(8,128)(2,1)}, bf16[8,256,256]{2,1,0:T(8,128)(2,1)S(1)}, u32[]{:S(2)}, u32[]{:S(2)}) collective-permute-start(bf16[8,256,256]{2,1,0:T(8,128)(2,1)} %collective-permute-done.4.refs_1_), channel_id=1, source_target_pairs={{0,8},{1,9},{2,10},{3,11},{4,12},{5,13},{6,14},{7,15},{8,0},{9,1},... | collective-permute-start | bytes 3145736 | tf_op jit(solution)/shard_map/ppermute | solution.py:289
  101.3 21.7 %collective-permute-start.20 = (bf16[2,512,256]{2,1,0:T(8,128)(2,1)S(1)}, bf16[2,512,256]{2,1,0:T(8,128)(2,1)S(1)}, u32[]{:S(2)}, u32[]{:S(2)}) collective-permute-start(bf16[2,512,256]{2,1,0:T(8,128)(2,1)S(1)} %add_convert_fusion), channel_id=1, source_target_pairs={{0,16},{1,17},{2,18},{3,19},{4,20},{5,21},{6,22},{7,23},{8,9},{9,8... | collective-permute-start | bytes 1572872 | tf_op jit(solution)/shard_map/ppermute | solution.py:289
  104.6 18.5 %copy-start.3 = (bf16[4,512,256]{2,1,0:T(8,128)(2,1)S(1)}, bf16[4,512,256]{2,1,0:T(8,128)(2,1)}, u32[]{:S(2)}) copy-start(bf16[4,512,256]{2,1,0:T(8,128)(2,1)} %copy-done.2) | copy-start | bytes 3145732
  104.6 40.7 %collective-permute-start.17 = (bf16[1,512,256]{2,1,0:T(8,128)(2,1)}, bf16[1,512,256]{2,1,0:T(8,128)(2,1)S(1)}, u32[]{:S(2)}, u32[]{:S(2)}) collective-permute-start(bf16[1,512,256]{2,1,0:T(8,128)(2,1)} %add_convert_fusion.4), channel_id=1, source_target_pairs={{0,4},{1,5},{2,6},{3,7},{4,0},{5,1},{6,2},{7,3},{8,12},{9,13},{10,... | collective-permute-start | bytes 786440 | tf_op jit(solution)/shard_map/ppermute | solution.py:289
  107.7 37.6 %collective-permute-start.25 = (bf16[1,512,256]{2,1,0:T(8,128)(2,1)}, bf16[1,512,256]{2,1,0:T(8,128)(2,1)}, u32[]{:S(2)}, u32[]{:S(2)}) collective-permute-start(bf16[1,512,256]{2,1,0:T(8,128)(2,1)} %add_convert_fusion.1), channel_id=1, source_target_pairs={{0,16},{1,17},{2,18},{3,19},{4,20},{5,21},{6,22},{7,23},{8,9},{9,8... | collective-permute-start | bytes 786440 | tf_op jit(solution)/shard_map/ppermute | solution.py:289
  125.1 20.1 %collective-permute-start.21 = (bf16[1,512,256]{2,1,0:T(8,128)(2,1)}, bf16[1,512,256]{2,1,0:T(8,128)(2,1)}, u32[]{:S(2)}, u32[]{:S(2)}) collective-permute-start(bf16[1,512,256]{2,1,0:T(8,128)(2,1)} %get-tuple-element.31), channel_id=1, source_target_pairs={{0,2},{1,3},{2,4},{3,5},{4,6},{5,7},{6,0},{7,1},{8,10},{9,11},{10,... | collective-permute-start | bytes 786440 | tf_op jit(solution)/shard_map/ppermute | solution.py:289
  125.1 20.1 %collective-permute-start.22 = (bf16[1,512,256]{2,1,0:T(8,128)(2,1)}, bf16[1,512,256]{2,1,0:T(8,128)(2,1)}, u32[]{:S(2)}, u32[]{:S(2)}) collective-permute-start(bf16[1,512,256]{2,1,0:T(8,128)(2,1)} %get-tuple-element.30), channel_id=1, source_target_pairs={{0,6},{1,7},{2,0},{3,1},{4,2},{5,3},{6,4},{7,5},{8,14},{9,15},{10,... | collective-permute-start | bytes 786440 | tf_op jit(solution)/shard_map/ppermute | solution.py:289
  144.6 0.7 copy-start.5
  145.3 0.9 copy-start.6
where the time goes:
time: 150 us
  Pallas kernels  60.1 us (40%)
  starting transfers between devices  40 us (27%)
  waiting for transfers between devices  35.6 us (24%)
  other arithmetic  7.21 us (5%)
  local copies, waits for them, and re-layouts  5.74 us (4%)
    ppermute x26, waiting for transfers between devices, send(): return lax.ppermute(value, AXES, pairs)  35.6 us
    ppermute x26, starting transfers between devices, send(): return lax.ppermute(value, AXES, pairs)  34.3 us
    pallas_call x2, Pallas kernels, project(): pl.pallas_call(functools.partial(project_kernel, devices // new_owner.sha...  29.8 us
    pallas_call x6, Pallas kernels, grad_blocks(): pl.pallas_call(functools.partial(grad_kernel, per_step, len(added), outs)...  24.9 us
    convert_element_type x5, other arithmetic, rounded_sum(): return total.astype(terms[0].dtype)  7.08 us
    all_to_all x1, starting transfers between devices, body(): lax.all_to_all(packed, AXES, split_axis=0, concat_axis=0, tiled=True)  5.67 us
    unnamed x32, local copies, waits for them, and re-layouts  4.95 us
    pallas_call x1, Pallas kernels, adam_rows(): pl.pallas_call(functools.partial(adam_kernel, len(weight_rows)), grid_spe...  3.41 us
  transfers between devices with their start and end apart: 27, of which 9 were waited for; matrix products, arithmetic and copies ran while one was open for 5% of the time, Pallas kernels for 32%

commit v1 on v0

--- a/solution.py
+++ b/solution.py
@@ -17,7 +17,7 @@
 
 AXES = ("rep", "fsdp")
 MIB = 1024 * 1024
-COLUMNS = 2
+COLUMNS = 1
 SUB = 8
 
 
@@ -126,10 +126,12 @@
 
 
 def project_kernel(groups, first, own, count, row_ref, old_ref, new_ref, token_ref, *refs):
-    piece_refs, (out_ref, rows_ref, held, logical, sems) = refs[:count], refs[-5:]
+    piece_refs, (out_ref, rows_ref, held, logical, total, sems) = refs[:count], refs[-6:]
     devices, row_block, _ = held.shape
-
-    @pl.when(pl.program_id(0) == 0)
+    step = pl.program_id(0)
+    blocks = logical.shape[0] // row_block
+
+    @pl.when(step == 0)
     def _():
         copies = []
         for piece_ref in piece_refs:
@@ -139,30 +141,34 @@
                 copies.append(pltpu.make_async_copy(piece_ref.at[index], target, sems.at[slot]))
         for copy in copies:
             copy.start()
+        total[...] = jnp.zeros_like(total)
         for copy in copies:
             copy.wait()
 
-        def place(pair, carry):
-            for block in range(0, devices, 2):
-                span = pl.ds(block * SUB, 2 * SUB)
-                top = held[2 * pair, span, :]
-                low = held[2 * pair + 1, span, :]
-                for half in range(2):
-                    part = slice(half * SUB, (half + 1) * SUB)
-                    start = (block + half) * row_block + pair * 2 * SUB
-                    logical[pl.ds(pl.multiple_of(start, 2 * SUB), 2 * SUB), :] = jnp.concatenate(
-                        [top[part], low[part]], axis=0
-                    )
-            return carry
-
-        lax.fori_loop(0, devices // 2, place, 0)
-        start = block_at(new_ref, groups, row_ref[own]) * row_block
-        start = pl.multiple_of(start, row_block)
+    for pair in range(devices // 2):
+        for block in range(0, blocks, 2):
+            span = pl.ds(pl.multiple_of((step * blocks + block) * SUB, 2 * SUB), 2 * SUB)
+            top = held[2 * pair, span, :]
+            low = held[2 * pair + 1, span, :]
+            for half in range(2):
+                part = slice(half * SUB, (half + 1) * SUB)
+                start = (block + half) * row_block + pair * 2 * SUB
+                logical[start : start + 2 * SUB, :] = jnp.concatenate(
+                    [top[part], low[part]], axis=0
+                )
+
+    block = block_at(new_ref, groups, row_ref[own])
+
+    @pl.when(lax.div(block, blocks) == step)
+    def _():
+        start = pl.multiple_of(lax.rem(block, blocks) * row_block, row_block)
         rows_ref[...] = logical[pl.ds(start, row_block), :]
 
-    out_ref[...] = jnp.dot(
-        token_ref[...], logical[...], preferred_element_type=jnp.float32
-    ).astype(out_ref.dtype)
+    total[...] += jnp.dot(token_ref[...], logical[...], preferred_element_type=jnp.float32)
+
+    @pl.when(step == pl.num_programs(0) - 1)
+    def _():
+        out_ref[...] = total[...].astype(out_ref.dtype)
 
 
 def project(tokens, pieces, row, first, own, old_owner, new_owner, part, parts, before):
@@ -170,23 +176,24 @@
     _, row_block, width = pieces[0].shape
     before = [] if before is None else [before]
     devices = old_owner.shape[0]
-    tile = rows // 4
+    tile = 4 * row_block
     return pl.pallas_call(
         functools.partial(
             project_kernel, devices // new_owner.shape[0], first, own, len(pieces)
         ),
         grid_spec=pltpu.PrefetchScalarGridSpec(
             num_scalar_prefetch=3,
-            grid=(rows // tile,),
-            in_specs=[pl.BlockSpec((tile, features), lambda i, *_: (i, 0))]
+            grid=(features // tile,),
+            in_specs=[pl.BlockSpec((rows, tile), lambda i, *_: (0, i))]
             + [pl.BlockSpec(memory_space=pl.ANY)] * (len(pieces) + len(before)),
             out_specs=[
-                pl.BlockSpec((tile, width), lambda i, *_: (i, part)),
+                pl.BlockSpec((rows, width), lambda i, *_: (0, part)),
                 pl.BlockSpec((row_block, width), lambda i, *_: (0, 0)),
             ],
             scratch_shapes=[
                 pltpu.VMEM((devices, row_block, width), jnp.bfloat16),
-                pltpu.VMEM((features, width), jnp.bfloat16),
+                pltpu.VMEM((tile, width), jnp.bfloat16),
+                pltpu.VMEM((rows, width), jnp.float32),
                 pltpu.SemaphoreType.DMA((devices,)),
             ],
         ),
@@ -300,7 +307,7 @@
 
 
 def shard_chunks(grid):
-    return [list(range(grid.far))]
+    return sum_chunks(grid)
 
 
 def tables(grid, devices):
@@ -391,7 +398,7 @@
     strip = row_block * width // devices
     grid = Grid(groups, shards)
     me = lax.axis_index(AXES)
-    by_tile = row_block == devices * SUB and width % 128 == 0 and devices % 2 == 0
+    by_tile = row_block == devices * SUB and width % 128 == 0 and devices % 4 == 0
 
     row = lax.dynamic_index_in_dim(jnp.asarray(tables(grid, devices)), me, 0, keepdims=False)
     per_far = grid.near * grid.side
@@ -414,8 +421,13 @@
     turned = cotangent.T
 
     waits = {}
-    if not by_tile:
-        waits = {}
+    if by_tile and len(marks) == 3:
+        waits = {
+            (1, 2): [packed, *marks[0][0]],
+            (1, 1): marks[1][2],
+            (1, 0): marks[0][1],
+            (0, 2): [*marks[2][2], *marks[1][0]],
+        }
     done = []
 
     def blocks_of(core, chunk, start, count, addend, cut):

time: 150 us -> 138 us (0.920)
  the two profiles are of different devices: /device:TPU:0 before, /device:TPU:8 now
where the time goes in v1:
time: 138 us
  waiting for transfers between devices  53.6 us (39%)
  Pallas kernels  46 us (33%)
  starting transfers between devices  26.4 us (19%)
  other arithmetic  5.97 us (4%)
  local copies, waits for them, and re-layouts  4.57 us (3%)
    ppermute x27, waiting for transfers between devices, send(): return lax.ppermute(value, AXES, pairs)  53.6 us
    pallas_call x6, Pallas kernels, grad_blocks(): pl.pallas_call(functools.partial(grad_kernel, per_step, len(added), outs)...  23.8 us
    ppermute x27, starting transfers between devices, send(): return lax.ppermute(value, AXES, pairs)  23 us
    pallas_call x1, Pallas kernels, project(): pl.pallas_call(functools.partial(project_kernel, devices // new_owner.sha...  18 us
    convert_element_type x5, other arithmetic, rounded_sum(): return total.astype(terms[0].dtype)  5.87 us
    all_to_all x1, starting transfers between devices, body(): lax.all_to_all(packed, AXES, split_axis=0, concat_axis=0, tiled=True)  3.37 us
    unnamed x28, local copies, waits for them, and re-layouts  3.02 us
  transfers between devices with their start and end apart: 28, of which 10 were waited for; matrix products, arithmetic and copies ran while one was open for 8% of the time, Pallas kernels for 28%

profile of v1, /device:TPU:8, one launch (start us, length us, event | category | flops | bytes accessed | tf_op | source)
XLA Modules:
  0.0 137.5 jit_solution(7265918100468874638)
XLA Ops:
  0.6 0.0 copy-start.5
  0.6 1.6 %collective-permute-start = (bf16[1,256,512]{2,1,0:T(8,128)(2,1)}, bf16[1,256,512]{2,1,0:T(8,128)(2,1)S(1)}, u32[]{:S(2)}, u32[]{:S(2)}) collective-permute-start(bf16[1,256,512]{2,1,0:T(8,128)(2,1)} %bitcast.10), channel_id=1, source_target_pairs={{0,16},{1,17},{2,18},{3,19},{4,20},{5,21},{6,22},{7,23},{8,9},{9,8... | collective-permute-start | bytes 786440 | tf_op jit(solution)/shard_map/ppermute | solution.py:296
  2.2 1.6 %collective-permute-start.4 = (bf16[1,256,512]{2,1,0:T(8,128)(2,1)}, bf16[1,256,512]{2,1,0:T(8,128)(2,1)S(1)}, u32[]{:S(2)}, u32[]{:S(2)}) collective-permute-start(bf16[1,256,512]{2,1,0:T(8,128)(2,1)} %bitcast.11), channel_id=1, source_target_pairs={{0,2},{1,3},{2,4},{3,5},{4,6},{5,7},{6,0},{7,1},{8,10},{9,11},{10,... | collective-permute-start | bytes 786440 | tf_op jit(solution)/shard_map/ppermute | solution.py:296
  3.8 0.4 collective-permute-start.5
  4.3 1.5 %copy.12 = bf16[1024,512]{0,1:T(8,128)(2,1)S(1)} copy(bf16[1024,512]{1,0:T(8,128)(2,1)} %param.9) | data formatting | bytes 2097152 | tf_op args[1]
  5.7 2.1 %pack_moments.1.refs_3_ = bf16[32,16,512]{2,1,0:T(8,128)(2,1)} custom-call(s32[8]{0:T(128)} %new_ref.15, f32[256,512]{1,0:T(8,128)} %first_ref.1, f32[256,512]{1,0:T(8,128)} %second_ref.1), custom_call_target="tpu_custom_call" | custom-call | bytes 1572864 | tf_op jit(solution)/shard_map/pack_moments/pallas_call | solution.py:114
  7.8 0.7 dynamic-slice_bitcast_fusion.row_ref
  8.5 3.3 %weight_gradient.6.refs_7_ = bf16[4,512,256]{2,1,0:T(8,128)(2,1)S(1)} custom-call(s32[64]{0:T(128)S(1)} %dynamic-slice_bitcast_fusion.row_ref, s32[8]{0:T(128)S(1)} %copy-done.5, bf16[1024,8192]{1,0:T(8,128)(2,1)} %refs_1_.11, bf16[1024,8192]{1,0:T(8,128)(2,1)} %refs_1_.11, bf16[512,1024]{1,0:T(8,128)(2,1)S(1)} %bitcast.4, ...), custom_call_target="tpu_custom_call" | custom-call | flops 1073741824 | bytes 4194304 | tf_op jit(solution)/shard_map/weight_gradient/pallas_call | solution.py:82
  11.8 0.0 copy-start.11
  11.8 0.0 collective-permute-done.4.refs_5_
  11.9 4.8 %collective-permute-done.5.refs_6_ = bf16[1,256,512]{2,1,0:T(8,128)(2,1)S(1)} collective-permute-done((bf16[1,256,512]{2,1,0:T(8,128)(2,1)}, bf16[1,256,512]{2,1,0:T(8,128)(2,1)S(1)}, u32[]{:S(2)}, u32[]{:S(2)}) %collective-permute-start.5) | collective-permute-done | bytes 262176 | tf_op jit(solution)/shard_map/ppermute | solution.py:296
  16.7 4.8 %weight_gradient.7.refs_4_ = bf16[8,512,256]{2,1,0:T(8,128)(2,1)S(1)} custom-call(s32[64]{0:T(128)S(1)} %dynamic-slice_bitcast_fusion.row_ref, s32[8]{0:T(128)S(1)} %copy-done.5, bf16[1024,8192]{1,0:T(8,128)(2,1)} %refs_1_.11, bf16[1024,8192]{1,0:T(8,128)(2,1)} %refs_1_.11, bf16[1024,8192]{1,0:T(8,128)(2,1)} %refs_1_.11, bf16[1024,8192]{1,0:T(8,128)(2,1)} %refs_1_.11, ...), custom_call_target="tpu_custom_call" | custom-call | flops 2147483648 | bytes 7340032 | tf_op jit(solution)/shard_map/weight_gradient/pallas_call | solution.py:82
  21.5 0.1 collective-permute-start.19
  21.6 0.5 collective-permute-start.15
  22.1 0.1 pad_maximum_fusion.refs_0_
  22.1 0.0 copy-start
  22.2 0.6 collective-permute-start.1
  22.8 0.1 pad_maximum_fusion.1
  22.8 1.6 %collective-permute-start.6 = (bf16[2,256,512]{2,1,0:T(8,128)(2,1)S(1)}, bf16[2,256,512]{2,1,0:T(8,128)(2,1)S(1)}, u32[]{:S(2)}, u32[]{:S(2)}) collective-permute-start(bf16[2,256,512]{2,1,0:T(8,128)(2,1)S(1)} %pad_maximum_fusion.1), channel_id=1, source_target_pairs={{0,16},{1,17},{2,18},{3,19},{4,20},{5,21},{6,22},{7,23},{8,9},{9,8... | collective-permute-start | bytes 1572872 | tf_op jit(solution)/shard_map/ppermute | solution.py:296
  24.4 1.7 %collective-permute-start.10 = (bf16[1,256,512]{2,1,0:T(8,128)(2,1)S(1)}, bf16[1,256,512]{2,1,0:T(8,128)(2,1)S(1)}, u32[]{:S(2)}, u32[]{:S(2)}) collective-permute-start(bf16[1,256,512]{2,1,0:T(8,128)(2,1)S(1)} %bitcast.14), channel_id=1, source_target_pairs={{0,4},{1,5},{2,6},{3,7},{4,0},{5,1},{6,2},{7,3},{8,12},{9,13},{10,... | collective-permute-start | bytes 786440 | tf_op jit(solution)/shard_map/ppermute | solution.py:296
  26.1 10.5 %collective-permute-done.1.refs_1_.refs_3_ = bf16[2,256,512]{2,1,0:T(8,128)(2,1)S(1)} collective-permute-done((bf16[2,256,512]{2,1,0:T(8,128)(2,1)S(1)}, bf16[2,256,512]{2,1,0:T(8,128)(2,1)S(1)}, u32[]{:S(2)}, u32[]{:S(2)}) %collective-permute-start.1) | collective-permute-done | bytes 524320 | tf_op jit(solution)/shard_map/ppermute | solution.py:296
  36.6 3.3 %weight_gradient.8.refs_6_ = bf16[4,512,256]{2,1,0:T(8,128)(2,1)S(1)} custom-call(s32[64]{0:T(128)S(1)} %dynamic-slice_bitcast_fusion.row_ref, s32[8]{0:T(128)S(1)} %copy-done.5, bf16[1024,8192]{1,0:T(8,128)(2,1)} %refs_1_.11, bf16[1024,8192]{1,0:T(8,128)(2,1)} %refs_1_.11, bf16[512,1024]{1,0:T(8,128)(2,1)S(1)} %bitcast.6, ...), custom_call_target="tpu_custom_call" | custom-call | flops 1073741824 | bytes 4194304 | tf_op jit(solution)/shard_map/weight_gradient/pallas_call | solution.py:82
  39.9 0.1 collective-permute-start.24
  40.0 0.0 collective-permute-done.6.refs_5_
  40.1 3.3 %weight_gradient.9 = (bf16[2,512,256]{2,1,0:T(8,128)(2,1)S(1)}, bf16[2,512,256]{2,1,0:T(8,128)(2,1)S(1)}) custom-call(s32[64]{0:T(128)S(1)} %dynamic-slice_bitcast_fusion.row_ref, s32[8]{0:T(128)S(1)} %copy-done.5, bf16[1024,8192]{1,0:T(8,128)(2,1)} %refs_1_.11, bf16[1024,8192]{1,0:T(8,128)(2,1)} %refs_1_.11, bf16[512,1024]{1,0:T(8,128)(2,1)S(1)} %bitcast.7, ...), custom_call_target="tpu_custom_call" | custom-call | flops 1073741824 | bytes 5242880 | tf_op jit(solution)/shard_map/weight_gradient/pallas_call | solution.py:82
  43.4 0.0 collective-permute-done.19.refs_5_
  43.4 4.9 %weight_gradient.10 = (bf16[4,512,256]{2,1,0:T(8,128)(2,1)S(1)}, bf16[4,512,256]{2,1,0:T(8,128)(2,1)S(1)}) custom-call(s32[64]{0:T(128)S(1)} %dynamic-slice_bitcast_fusion.row_ref, s32[8]{0:T(128)S(1)} %copy-done.5, bf16[1024,8192]{1,0:T(8,128)(2,1)} %refs_1_.11, bf16[1024,8192]{1,0:T(8,128)(2,1)} %refs_1_.11, bf16[1024,8192]{1,0:T(8,128)(2,1)} %refs_1_.11, ...), custom_call_target="tpu_custom_call" | custom-call | flops 2147483648 | bytes 9437184 | tf_op jit(solution)/shard_map/weight_gradient/pallas_call | solution.py:82
  48.3 0.6 collective-permute-start.20
  48.9 0.8 constant_dynamic-update-slice_fusion.2
  49.6 0.7 constant_dynamic-update-slice_fusion.1
  50.4 0.8 constant_dynamic-update-slice_fusion.refs_4_
  51.2 1.5 %collective-permute-start.7 = (bf16[4,256,512]{2,1,0:T(8,128)(2,1)}, bf16[4,256,512]{2,1,0:T(8,128)(2,1)}, u32[]{:S(2)}, u32[]{:S(2)}) collective-permute-start(bf16[4,256,512]{2,1,0:T(8,128)(2,1)} %constant_dynamic-update-slice_fusion.refs_4_), channel_id=1, source_target_pairs={{0,1},{1,0},{2,3},{3,2},{4,5},{5,4},{6,7},{7,6},{8,24},{9,25},{10,... | collective-permute-start | bytes 3145736 | tf_op jit(solution)/shard_map/ppermute | solution.py:296
  52.7 1.4 %collective-permute-start.11 = (bf16[1,256,512]{2,1,0:T(8,128)(2,1)S(1)}, bf16[1,256,512]{2,1,0:T(8,128)(2,1)S(1)}, u32[]{:S(2)}, u32[]{:S(2)}) collective-permute-start(bf16[1,256,512]{2,1,0:T(8,128)(2,1)S(1)} %collective-permute-done.10.refs_4_), channel_id=1, source_target_pairs={{0,16},{1,17},{2,18},{3,19},{4,20},{5,21},{6,22},{7,23},{8,9},{9,8... | collective-permute-start | bytes 786440 | tf_op jit(solution)/shard_map/ppermute | solution.py:296
  54.1 0.0 collective-permute-start.2
  54.1 7.9 %collective-permute-done.11 = bf16[1,256,512]{2,1,0:T(8,128)(2,1)S(1)} collective-permute-done((bf16[1,256,512]{2,1,0:T(8,128)(2,1)S(1)}, bf16[1,256,512]{2,1,0:T(8,128)(2,1)S(1)}, u32[]{:S(2)}, u32[]{:S(2)}) %collective-permute-start.11) | collective-permute-done | bytes 262176 | tf_op jit(solution)/shard_map/ppermute | solution.py:296
  61.9 0.5 collective-permute-start.16
  62.5 1.6 %collective-permute-start.12 = (bf16[2,256,512]{2,1,0:T(8,128)(2,1)S(1)}, bf16[2,256,512]{2,1,0:T(8,128)(2,1)}, u32[]{:S(2)}, u32[]{:S(2)}) collective-permute-start(bf16[2,256,512]{2,1,0:T(8,128)(2,1)S(1)} %constant_dynamic-update-slice_fusion.3.refs_8_), channel_id=1, source_target_pairs={{0,1},{1,0},{2,3},{3,2},{4,5},{5,4},{6,7},{7,6},{8,24},{9,25},{10,... | collective-permute-start | bytes 1572872 | tf_op jit(solution)/shard_map/ppermute | solution.py:296
  64.1 4.1 %weight_gradient.11 = (bf16[2,512,256]{2,1,0:T(8,128)(2,1)}, bf16[2,512,256]{2,1,0:T(8,128)(2,1)S(1)}) custom-call(s32[64]{0:T(128)S(1)} %dynamic-slice_bitcast_fusion.row_ref, s32[8]{0:T(128)S(1)} %copy-done.5, bf16[1024,8192]{1,0:T(8,128)(2,1)} %refs_1_.11, bf16[1024,8192]{1,0:T(8,128)(2,1)} %refs_1_.11, bf16[512,1024]{1,0:T(8,128)(2,1)S(1)} %bitcast.9, ...), custom_call_target="tpu_custom_call" | custom-call | flops 1073741824 | bytes 5242880 | tf_op jit(solution)/shard_map/weight_gradient/pallas_call | solution.py:82
  68.2 0.6 collective-permute-start.25
  68.8 1.0 add_convert_fusion
  69.8 1.4 %collective-permute-start.21 = (bf16[2,512,256]{2,1,0:T(8,128)(2,1)}, bf16[2,512,256]{2,1,0:T(8,128)(2,1)}, u32[]{:S(2)}, u32[]{:S(2)}) collective-permute-start(bf16[2,512,256]{2,1,0:T(8,128)(2,1)} %add_convert_fusion), channel_id=1, source_target_pairs={{0,16},{1,17},{2,18},{3,19},{4,20},{5,21},{6,22},{7,23},{8,9},{9,8... | collective-permute-start | bytes 1572872 | tf_op jit(solution)/shard_map/ppermute | solution.py:296
  71.1 11.7 %collective-permute-done.7.refs_5_ = bf16[4,256,512]{2,1,0:T(8,128)(2,1)} collective-permute-done((bf16[4,256,512]{2,1,0:T(8,128)(2,1)}, bf16[4,256,512]{2,1,0:T(8,128)(2,1)}, u32[]{:S(2)}, u32[]{:S(2)}) %collective-permute-start.7) | collective-permute-done | bytes 1048608 | tf_op jit(solution)/shard_map/ppermute | solution.py:296
  82.8 5.6 %collective-permute-done.16 = bf16[2,512,256]{2,1,0:T(8,128)(2,1)S(1)} collective-permute-done((bf16[2,512,256]{2,1,0:T(8,128)(2,1)S(1)}, bf16[2,512,256]{2,1,0:T(8,128)(2,1)S(1)}, u32[]{:S(2)}, u32[]{:S(2)}) %collective-permute-start.16) | collective-permute-done | bytes 524320 | tf_op jit(solution)/shard_map/ppermute | solution.py:296
  88.4 0.1 add_convert_fusion.5
  88.5 5.6 %collective-permute-done.12.refs_9_ = bf16[2,256,512]{2,1,0:T(8,128)(2,1)} collective-permute-done((bf16[2,256,512]{2,1,0:T(8,128)(2,1)S(1)}, bf16[2,256,512]{2,1,0:T(8,128)(2,1)}, u32[]{:S(2)}, u32[]{:S(2)}) %collective-permute-start.12) | collective-permute-done | bytes 524320 | tf_op jit(solution)/shard_map/ppermute | solution.py:296
  94.2 1.4 %collective-permute-start.17 = (bf16[1,512,256]{2,1,0:T(8,128)(2,1)S(1)}, bf16[1,512,256]{2,1,0:T(8,128)(2,1)}, u32[]{:S(2)}, u32[]{:S(2)}) collective-permute-start(bf16[1,512,256]{2,1,0:T(8,128)(2,1)S(1)} %add_convert_fusion.5), channel_id=1, source_target_pairs={{0,16},{1,17},{2,18},{3,19},{4,20},{5,21},{6,22},{7,23},{8,9},{9,8... | collective-permute-start | bytes 786440 | tf_op jit(solution)/shard_map/ppermute | solution.py:296
  95.6 3.4 %all-to-all-start = ((bf16[32,16,512]{2,1,0:T(8,128)(2,1)}), bf16[32,16,512]{2,1,0:T(8,128)(2,1)S(1)}, u32[]{:S(2)}, u32[]{:S(2)}) async-start(bf16[32,16,512]{2,1,0:T(8,128)(2,1)} %pack_moments.1.refs_3_), calls=%async_computation | async-start | bytes 1048576 | tf_op jit(solution)/shard_map/all_to_all | solution.py:419
  99.0 0.0 copy-start.1
  99.0 0.0 copy-start.6
  99.0 0.0 copy-start.8
  99.0 3.3 %collective-permute-done.17 = bf16[1,512,256]{2,1,0:T(8,128)(2,1)} collective-permute-done((bf16[1,512,256]{2,1,0:T(8,128)(2,1)S(1)}, bf16[1,512,256]{2,1,0:T(8,128)(2,1)}, u32[]{:S(2)}, u32[]{:S(2)}) %collective-permute-start.17) | collective-permute-done | bytes 262176 | tf_op jit(solution)/shard_map/ppermute | solution.py:296
  102.4 1.0 collective-permute-done.25.refs_5_
  103.4 0.5 collective-permute-start.14
  103.9 1.9 %add_convert_fusion.4 = bf16[1,512,256]{2,1,0:T(8,128)(2,1)} fusion(bf16[1,512,256]{2,1,0:T(8,128)(2,1)} %collective-permute-done.17, bf16[2,512,256]{2,1,0:T(8,128)(2,1)} %copy-done.10, bf16[2,512,256]{2,1,0:T(8,128)(2,1)} %copy-done.2), kind=kLoop, calls=%fused_computation.6 | loop fusion | flops 786432 | bytes 1048576 | tf_op jit(solution)/shard_map/convert_element_type | solution.py:301
  105.8 0.8 add_convert_fusion.1
  106.5 2.2 %add_convert_fusion.2 = (bf16[1,512,256]{2,1,0:T(8,128)(2,1)}, bf16[1,512,256]{2,1,0:T(8,128)(2,1)}) fusion(bf16[2,512,256]{2,1,0:T(8,128)(2,1)} %collective-permute-done.21, bf16[4,512,256]{2,1,0:T(8,128)(2,1)} %copy-done.9, bf16[4,512,256]{2,1,0:T(8,128)(2,1)S(1)} %get-tuple-element.19), kind=kLoop, calls=%fused_computation.4 | loop fusion | flops 1572864 | bytes 2097152 | tf_op jit(solution)/shard_map/convert_element_type | solution.py:301
  108.7 2.0 %collective-permute-start.18 = (bf16[1,512,256]{2,1,0:T(8,128)(2,1)}, bf16[1,512,256]{2,1,0:T(8,128)(2,1)S(1)}, u32[]{:S(2)}, u32[]{:S(2)}) collective-permute-start(bf16[1,512,256]{2,1,0:T(8,128)(2,1)} %add_convert_fusion.4), channel_id=1, source_target_pairs={{0,4},{1,5},{2,6},{3,7},{4,0},{5,1},{6,2},{7,3},{8,12},{9,13},{10,... | collective-permute-start | bytes 786440 | tf_op jit(solution)/shard_map/ppermute | solution.py:296
  110.8 1.3 collective-permute-start.26
  112.0 0.9 collective-permute-start.22
  112.9 1.2 collective-permute-start.23
  114.1 18.0 %project.1 = (bf16[1024,512]{1,0:T(8,128)(2,1)}, bf16[256,512]{1,0:T(8,128)(2,1)S(1)}) custom-call(s32[64]{0:T(128)S(1)} %dynamic-slice_bitcast_fusion.row_ref, s32[32]{0:T(128)S(1)} %copy-done.6, s32[8]{0:T(128)S(1)} %copy-done.5, bf16[1024,8192]{1,0:T(8,128)(2,1)} %refs_1_.11, bf16[2,256,512]{2,1,0:T(8,128)(2,1)S(1)} %copy-done.1, ...), custom_call_target="tpu_custom_call" | custom-call | flops 8589934592 | bytes 26214400 | tf_op jit(solution)/shard_map/project/pallas_call | solution.py:180
  132.1 1.2 collective-permute-done.22.refs_2_
  133.3 2.0 %collective-permute-done.23.refs_3_ = bf16[1,512,256]{2,1,0:T(8,128)(2,1)S(1)} collective-permute-done((bf16[1,512,256]{2,1,0:T(8,128)(2,1)}, bf16[1,512,256]{2,1,0:T(8,128)(2,1)S(1)}, u32[]{:S(2)}, u32[]{:S(2)}) %collective-permute-start.23) | collective-permute-done | bytes 262176 | tf_op jit(solution)/shard_map/ppermute | solution.py:296
  135.3 2.2 %adam_rows.1 = (bf16[256,512]{1,0:T(8,128)(2,1)}, f32[256,512]{1,0:T(8,128)}, f32[256,512]{1,0:T(8,128)}) custom-call(s32[32]{0:T(128)S(1)} %copy-done.6, bf16[32,16,512]{2,1,0:T(8,128)(2,1)S(1)} %all-to-all-done.moments_ref, bf16[256,512]{1,0:T(8,128)(2,1)S(1)} %get-tuple-element.16.refs_0_, bf16[1,512,256]{2,1,0:T(8,128)(2,1)S(1)} %collective-permute-done.18.refs_1_, ...), custom_call_target="tpu_custom_call" | custom-call | flops 2621440 | bytes 2097152 | tf_op jit(solution)/shard_map/adam_rows/pallas_call | solution.py:248
  (39 shorter events, 0.1 us)
Async XLA Ops:
  0.6 7.9 %copy-start.5 = (s32[8]{0:T(128)S(1)}, s32[8]{0:T(128)}, u32[]{:S(2)}) copy-start(s32[8]{0:T(128)} %new_ref.15) | copy-start | bytes 100
  0.6 7.9 %collective-permute-start = (bf16[1,256,512]{2,1,0:T(8,128)(2,1)}, bf16[1,256,512]{2,1,0:T(8,128)(2,1)S(1)}, u32[]{:S(2)}, u32[]{:S(2)}) collective-permute-start(bf16[1,256,512]{2,1,0:T(8,128)(2,1)} %bitcast.10), channel_id=1, source_target_pairs={{0,16},{1,17},{2,18},{3,19},{4,20},{5,21},{6,22},{7,23},{8,9},{9,8... | collective-permute-start | bytes 786440 | tf_op jit(solution)/shard_map/ppermute | solution.py:296
  2.2 9.6 %collective-permute-start.4 = (bf16[1,256,512]{2,1,0:T(8,128)(2,1)}, bf16[1,256,512]{2,1,0:T(8,128)(2,1)S(1)}, u32[]{:S(2)}, u32[]{:S(2)}) collective-permute-start(bf16[1,256,512]{2,1,0:T(8,128)(2,1)} %bitcast.11), channel_id=1, source_target_pairs={{0,2},{1,3},{2,4},{3,5},{4,6},{5,7},{6,0},{7,1},{8,10},{9,11},{10,... | collective-permute-start | bytes 786440 | tf_op jit(solution)/shard_map/ppermute | solution.py:296
  3.8 12.9 %collective-permute-start.5 = (bf16[1,256,512]{2,1,0:T(8,128)(2,1)}, bf16[1,256,512]{2,1,0:T(8,128)(2,1)S(1)}, u32[]{:S(2)}, u32[]{:S(2)}) collective-permute-start(bf16[1,256,512]{2,1,0:T(8,128)(2,1)} %bitcast.12), channel_id=1, source_target_pairs={{0,6},{1,7},{2,0},{3,1},{4,2},{5,3},{6,4},{7,5},{8,14},{9,15},{10,... | collective-permute-start | bytes 786440 | tf_op jit(solution)/shard_map/ppermute | solution.py:296
  11.8 10.3 %copy-start.11 = (bf16[256,512]{1,0:T(8,128)(2,1)S(1)}, bf16[256,512]{1,0:T(8,128)(2,1)}, u32[]{:S(2)}) copy-start(bf16[256,512]{1,0:T(8,128)(2,1)} %param.10) | copy-start | bytes 786436
  21.5 21.9 %collective-permute-start.19 = (bf16[8,512,256]{2,1,0:T(8,128)(2,1)S(1)}, bf16[8,512,256]{2,1,0:T(8,128)(2,1)S(1)}, u32[]{:S(2)}, u32[]{:S(2)}) collective-permute-start(bf16[8,512,256]{2,1,0:T(8,128)(2,1)S(1)} %weight_gradient.7.refs_4_), channel_id=1, source_target_pairs={{0,8},{1,9},{2,10},{3,11},{4,12},{5,13},{6,14},{7,15},{8,0},{9,1},... | collective-permute-start | bytes 6291464 | tf_op jit(solution)/shard_map/ppermute | solution.py:296
  21.6 18.4 %collective-permute-start.15 = (bf16[4,512,256]{2,1,0:T(8,128)(2,1)S(1)}, bf16[4,512,256]{2,1,0:T(8,128)(2,1)S(1)}, u32[]{:S(2)}, u32[]{:S(2)}) collective-permute-start(bf16[4,512,256]{2,1,0:T(8,128)(2,1)S(1)} %weight_gradient.6.refs_7_), channel_id=1, source_target_pairs={{0,8},{1,9},{2,10},{3,11},{4,12},{5,13},{6,14},{7,15},{8,0},{9,1},... | collective-permute-start | bytes 3145736 | tf_op jit(solution)/shard_map/ppermute | solution.py:296
  22.1 31.9 %copy-start = (bf16[2,256,512]{2,1,0:T(8,128)(2,1)}, bf16[2,256,512]{2,1,0:T(8,128)(2,1)S(1)}, u32[]{:S(2)}) copy-start(bf16[2,256,512]{2,1,0:T(8,128)(2,1)S(1)} %pad_maximum_fusion.refs_0_) | copy-start | bytes 1572868
  22.2 14.5 %collective-permute-start.1 = (bf16[2,256,512]{2,1,0:T(8,128)(2,1)S(1)}, bf16[2,256,512]{2,1,0:T(8,128)(2,1)S(1)}, u32[]{:S(2)}, u32[]{:S(2)}) collective-permute-start(bf16[2,256,512]{2,1,0:T(8,128)(2,1)S(1)} %pad_maximum_fusion.refs_0_), channel_id=1, source_target_pairs={{0,1},{1,0},{2,3},{3,2},{4,5},{5,4},{6,7},{7,6},{8,24},{9,25},{10,... | collective-permute-start | bytes 1572872 | tf_op jit(solution)/shard_map/ppermute | solution.py:296
  22.8 17.2 %collective-permute-start.6 = (bf16[2,256,512]{2,1,0:T(8,128)(2,1)S(1)}, bf16[2,256,512]{2,1,0:T(8,128)(2,1)S(1)}, u32[]{:S(2)}, u32[]{:S(2)}) collective-permute-start(bf16[2,256,512]{2,1,0:T(8,128)(2,1)S(1)} %pad_maximum_fusion.1), channel_id=1, source_target_pairs={{0,16},{1,17},{2,18},{3,19},{4,20},{5,21},{6,22},{7,23},{8,9},{9,8... | collective-permute-start | bytes 1572872 | tf_op jit(solution)/shard_map/ppermute | solution.py:296
  24.4 15.6 %collective-permute-start.10 = (bf16[1,256,512]{2,1,0:T(8,128)(2,1)S(1)}, bf16[1,256,512]{2,1,0:T(8,128)(2,1)S(1)}, u32[]{:S(2)}, u32[]{:S(2)}) collective-permute-start(bf16[1,256,512]{2,1,0:T(8,128)(2,1)S(1)} %bitcast.14), channel_id=1, source_target_pairs={{0,4},{1,5},{2,6},{3,7},{4,0},{5,1},{6,2},{7,3},{8,12},{9,13},{10,... | collective-permute-start | bytes 786440 | tf_op jit(solution)/shard_map/ppermute | solution.py:296
  39.9 22.6 %collective-permute-start.24 = (bf16[4,512,256]{2,1,0:T(8,128)(2,1)S(1)}, bf16[4,512,256]{2,1,0:T(8,128)(2,1)S(1)}, u32[]{:S(2)}, u32[]{:S(2)}) collective-permute-start(bf16[4,512,256]{2,1,0:T(8,128)(2,1)S(1)} %weight_gradient.8.refs_6_), channel_id=1, source_target_pairs={{0,8},{1,9},{2,10},{3,11},{4,12},{5,13},{6,14},{7,15},{8,0},{9,1},... | collective-permute-start | bytes 3145736 | tf_op jit(solution)/shard_map/ppermute | solution.py:296
  43.4 45.1 %copy-start.2 = (bf16[2,512,256]{2,1,0:T(8,128)(2,1)}, bf16[2,512,256]{2,1,0:T(8,128)(2,1)S(1)}, u32[]{:S(2)}) copy-start(bf16[2,512,256]{2,1,0:T(8,128)(2,1)S(1)} %get-tuple-element.17) | copy-start | bytes 1572868
  48.3 19.9 %collective-permute-start.20 = (bf16[4,512,256]{2,1,0:T(8,128)(2,1)S(1)}, bf16[4,512,256]{2,1,0:T(8,128)(2,1)S(1)}, u32[]{:S(2)}, u32[]{:S(2)}) collective-permute-start(bf16[4,512,256]{2,1,0:T(8,128)(2,1)S(1)} %get-tuple-element.20.refs_4_), channel_id=1, source_target_pairs={{0,1},{1,0},{2,3},{3,2},{4,5},{5,4},{6,7},{7,6},{8,24},{9,25},{10,... | collective-permute-start | bytes 3145736 | tf_op jit(solution)/shard_map/ppermute | solution.py:296
  51.2 31.6 %collective-permute-start.7 = (bf16[4,256,512]{2,1,0:T(8,128)(2,1)}, bf16[4,256,512]{2,1,0:T(8,128)(2,1)}, u32[]{:S(2)}, u32[]{:S(2)}) collective-permute-start(bf16[4,256,512]{2,1,0:T(8,128)(2,1)} %constant_dynamic-update-slice_fusion.refs_4_), channel_id=1, source_target_pairs={{0,1},{1,0},{2,3},{3,2},{4,5},{5,4},{6,7},{7,6},{8,24},{9,25},{10,... | collective-permute-start | bytes 3145736 | tf_op jit(solution)/shard_map/ppermute | solution.py:296
  52.7 9.2 %collective-permute-start.11 = (bf16[1,256,512]{2,1,0:T(8,128)(2,1)S(1)}, bf16[1,256,512]{2,1,0:T(8,128)(2,1)S(1)}, u32[]{:S(2)}, u32[]{:S(2)}) collective-permute-start(bf16[1,256,512]{2,1,0:T(8,128)(2,1)S(1)} %collective-permute-done.10.refs_4_), channel_id=1, source_target_pairs={{0,16},{1,17},{2,18},{3,19},{4,20},{5,21},{6,22},{7,23},{8,9},{9,8... | collective-permute-start | bytes 786440 | tf_op jit(solution)/shard_map/ppermute | solution.py:296
  54.1 15.7 %collective-permute-start.2 = (bf16[2,256,512]{2,1,0:T(8,128)(2,1)S(1)}, bf16[2,256,512]{2,1,0:T(8,128)(2,1)S(1)}, u32[]{:S(2)}, u32[]{:S(2)}) collective-permute-start(bf16[2,256,512]{2,1,0:T(8,128)(2,1)S(1)} %pad_maximum_fusion.refs_0_), channel_id=1, source_target_pairs={{0,8},{1,9},{2,10},{3,11},{4,12},{5,13},{6,14},{7,15},{8,0},{9,1},... | collective-permute-start | bytes 1572872 | tf_op jit(solution)/shard_map/ppermute | solution.py:296
  61.9 26.5 %collective-permute-start.16 = (bf16[2,512,256]{2,1,0:T(8,128)(2,1)S(1)}, bf16[2,512,256]{2,1,0:T(8,128)(2,1)S(1)}, u32[]{:S(2)}, u32[]{:S(2)}) collective-permute-start(bf16[2,512,256]{2,1,0:T(8,128)(2,1)S(1)} %get-tuple-element.18.refs_6_), channel_id=1, source_target_pairs={{0,1},{1,0},{2,3},{3,2},{4,5},{5,4},{6,7},{7,6},{8,24},{9,25},{10,... | collective-permute-start | bytes 1572872 | tf_op jit(solution)/shard_map/ppermute | solution.py:296
  62.5 5.7 %copy-start.3 = (bf16[2,256,512]{2,1,0:T(8,128)(2,1)}, bf16[2,256,512]{2,1,0:T(8,128)(2,1)S(1)}, u32[]{:S(2)}) copy-start(bf16[2,256,512]{2,1,0:T(8,128)(2,1)S(1)} %constant_dynamic-update-slice_fusion.3.refs_8_) | copy-start | bytes 1572868
  62.5 31.6 %collective-permute-start.12 = (bf16[2,256,512]{2,1,0:T(8,128)(2,1)S(1)}, bf16[2,256,512]{2,1,0:T(8,128)(2,1)}, u32[]{:S(2)}, u32[]{:S(2)}) collective-permute-start(bf16[2,256,512]{2,1,0:T(8,128)(2,1)S(1)} %constant_dynamic-update-slice_fusion.3.refs_8_), channel_id=1, source_target_pairs={{0,1},{1,0},{2,3},{3,2},{4,5},{5,4},{6,7},{7,6},{8,24},{9,25},{10,... | collective-permute-start | bytes 1572872 | tf_op jit(solution)/shard_map/ppermute | solution.py:296
  68.2 26.0 %copy-start.9 = (bf16[4,512,256]{2,1,0:T(8,128)(2,1)}, bf16[4,512,256]{2,1,0:T(8,128)(2,1)S(1)}, u32[]{:S(2)}) copy-start(bf16[4,512,256]{2,1,0:T(8,128)(2,1)S(1)} %collective-permute-done.20) | copy-start | bytes 3145732
  68.2 35.2 %collective-permute-start.25 = (bf16[2,512,256]{2,1,0:T(8,128)(2,1)}, bf16[2,512,256]{2,1,0:T(8,128)(2,1)S(1)}, u32[]{:S(2)}, u32[]{:S(2)}) collective-permute-start(bf16[2,512,256]{2,1,0:T(8,128)(2,1)} %get-tuple-element.22), channel_id=1, source_target_pairs={{0,1},{1,0},{2,3},{3,2},{4,5},{5,4},{6,7},{7,6},{8,24},{9,25},{10,... | collective-permute-start | bytes 1572872 | tf_op jit(solution)/shard_map/ppermute | solution.py:296
  69.8 24.4 %copy-start.7 = (bf16[2,256,512]{2,1,0:T(8,128)(2,1)}, bf16[2,256,512]{2,1,0:T(8,128)(2,1)S(1)}, u32[]{:S(2)}) copy-start(bf16[2,256,512]{2,1,0:T(8,128)(2,1)S(1)} %collective-permute-done.2.refs_2_) | copy-start | bytes 1572868
  69.8 33.6 %collective-permute-start.21 = (bf16[2,512,256]{2,1,0:T(8,128)(2,1)}, bf16[2,512,256]{2,1,0:T(8,128)(2,1)}, u32[]{:S(2)}, u32[]{:S(2)}) collective-permute-start(bf16[2,512,256]{2,1,0:T(8,128)(2,1)} %add_convert_fusion), channel_id=1, source_target_pairs={{0,16},{1,17},{2,18},{3,19},{4,20},{5,21},{6,22},{7,23},{8,9},{9,8... | collective-permute-start | bytes 1572872 | tf_op jit(solution)/shard_map/ppermute | solution.py:296
  82.8 30.1 %collective-permute-start.8 = (bf16[4,256,512]{2,1,0:T(8,128)(2,1)}, bf16[4,256,512]{2,1,0:T(8,128)(2,1)}, u32[]{:S(2)}, u32[]{:S(2)}) collective-permute-start(bf16[4,256,512]{2,1,0:T(8,128)(2,1)} %constant_dynamic-update-slice_fusion.refs_4_), channel_id=1, source_target_pairs={{0,8},{1,9},{2,10},{3,11},{4,12},{5,13},{6,14},{7,15},{8,0},{9,1},... | collective-permute-start | bytes 3145736 | tf_op jit(solution)/shard_map/ppermute | solution.py:296
  88.4 5.7 %copy-start.10 = (bf16[2,512,256]{2,1,0:T(8,128)(2,1)}, bf16[2,512,256]{2,1,0:T(8,128)(2,1)S(1)}, u32[]{:S(2)}) copy-start(bf16[2,512,256]{2,1,0:T(8,128)(2,1)S(1)} %collective-permute-done.16) | copy-start | bytes 1572868
  88.4 25.6 %collective-permute-start.9 = (bf16[4,256,512]{2,1,0:T(8,128)(2,1)}, bf16[4,256,512]{2,1,0:T(8,128)(2,1)}, u32[]{:S(2)}, u32[]{:S(2)}) collective-permute-start(bf16[4,256,512]{2,1,0:T(8,128)(2,1)} %collective-permute-done.7.refs_5_), channel_id=1, source_target_pairs={{0,8},{1,9},{2,10},{3,11},{4,12},{5,13},{6,14},{7,15},{8,0},{9,1},... | collective-permute-start | bytes 3145736 | tf_op jit(solution)/shard_map/ppermute | solution.py:296
  94.2 8.2 %collective-permute-start.17 = (bf16[1,512,256]{2,1,0:T(8,128)(2,1)S(1)}, bf16[1,512,256]{2,1,0:T(8,128)(2,1)}, u32[]{:S(2)}, u32[]{:S(2)}) collective-permute-start(bf16[1,512,256]{2,1,0:T(8,128)(2,1)S(1)} %add_convert_fusion.5), channel_id=1, source_target_pairs={{0,16},{1,17},{2,18},{3,19},{4,20},{5,21},{6,22},{7,23},{8,9},{9,8... | collective-permute-start | bytes 786440 | tf_op jit(solution)/shard_map/ppermute | solution.py:296
  95.6 36.5 %all-to-all-start = ((bf16[32,16,512]{2,1,0:T(8,128)(2,1)}), bf16[32,16,512]{2,1,0:T(8,128)(2,1)S(1)}, u32[]{:S(2)}, u32[]{:S(2)}) async-start(bf16[32,16,512]{2,1,0:T(8,128)(2,1)} %pack_moments.1.refs_3_), calls=%async_computation | async-start | bytes 1048576 | tf_op jit(solution)/shard_map/all_to_all | solution.py:419
  99.0 15.1 %copy-start.1 = (bf16[2,256,512]{2,1,0:T(8,128)(2,1)S(1)}, bf16[2,256,512]{2,1,0:T(8,128)(2,1)}, u32[]{:S(2)}) copy-start(bf16[2,256,512]{2,1,0:T(8,128)(2,1)} %copy-done) | copy-start | bytes 1572868
  99.0 15.1 %copy-start.4 = (bf16[2,256,512]{2,1,0:T(8,128)(2,1)S(1)}, bf16[2,256,512]{2,1,0:T(8,128)(2,1)}, u32[]{:S(2)}) copy-start(bf16[2,256,512]{2,1,0:T(8,128)(2,1)} %copy-done.3) | copy-start | bytes 1572868
  99.0 15.1 %copy-start.6 = (s32[32]{0:T(128)S(1)}, s32[32]{0:T(128)}, u32[]{:S(2)}) copy-start(s32[32]{0:T(128)} %owner_ref.1) | copy-start | bytes 388
  99.0 15.1 %copy-start.8 = (bf16[2,256,512]{2,1,0:T(8,128)(2,1)S(1)}, bf16[2,256,512]{2,1,0:T(8,128)(2,1)}, u32[]{:S(2)}) copy-start(bf16[2,256,512]{2,1,0:T(8,128)(2,1)} %copy-done.7) | copy-start | bytes 1572868
  102.4 6.3 %collective-permute-start.13 = (bf16[2,256,512]{2,1,0:T(8,128)(2,1)}, bf16[2,256,512]{2,1,0:T(8,128)(2,1)S(1)}, u32[]{:S(2)}, u32[]{:S(2)}) collective-permute-start(bf16[2,256,512]{2,1,0:T(8,128)(2,1)} %copy-done.3), channel_id=1, source_target_pairs={{0,8},{1,9},{2,10},{3,11},{4,12},{5,13},{6,14},{7,15},{8,0},{9,1},... | collective-permute-start | bytes 1572872 | tf_op jit(solution)/shard_map/ppermute | solution.py:296
  103.4 7.4 %collective-permute-start.3 = (bf16[2,256,512]{2,1,0:T(8,128)(2,1)S(1)}, bf16[2,256,512]{2,1,0:T(8,128)(2,1)S(1)}, u32[]{:S(2)}, u32[]{:S(2)}) collective-permute-start(bf16[2,256,512]{2,1,0:T(8,128)(2,1)S(1)} %collective-permute-done.1.refs_1_.refs_3_), channel_id=1, source_target_pairs={{0,8},{1,9},{2,10},{3,11},{4,12},{5,13},{6,14},{7,15},{8,0},{9,1},... | collective-permute-start | bytes 1572872 | tf_op jit(solution)/shard_map/ppermute | solution.py:296
  103.4 8.7 %collective-permute-start.14 = (bf16[2,256,512]{2,1,0:T(8,128)(2,1)}, bf16[2,256,512]{2,1,0:T(8,128)(2,1)S(1)}, u32[]{:S(2)}, u32[]{:S(2)}) collective-permute-start(bf16[2,256,512]{2,1,0:T(8,128)(2,1)} %collective-permute-done.12.refs_9_), channel_id=1, source_target_pairs={{0,8},{1,9},{2,10},{3,11},{4,12},{5,13},{6,14},{7,15},{8,0},{9,1},... | collective-permute-start | bytes 1572872 | tf_op jit(solution)/shard_map/ppermute | solution.py:296
  108.7 23.4 %collective-permute-start.18 = (bf16[1,512,256]{2,1,0:T(8,128)(2,1)}, bf16[1,512,256]{2,1,0:T(8,128)(2,1)S(1)}, u32[]{:S(2)}, u32[]{:S(2)}) collective-permute-start(bf16[1,512,256]{2,1,0:T(8,128)(2,1)} %add_convert_fusion.4), channel_id=1, source_target_pairs={{0,4},{1,5},{2,6},{3,7},{4,0},{5,1},{6,2},{7,3},{8,12},{9,13},{10,... | collective-permute-start | bytes 786440 | tf_op jit(solution)/shard_map/ppermute | solution.py:296
  110.8 21.4 %collective-permute-start.26 = (bf16[1,512,256]{2,1,0:T(8,128)(2,1)}, bf16[1,512,256]{2,1,0:T(8,128)(2,1)S(1)}, u32[]{:S(2)}, u32[]{:S(2)}) collective-permute-start(bf16[1,512,256]{2,1,0:T(8,128)(2,1)} %add_convert_fusion.1), channel_id=1, source_target_pairs={{0,16},{1,17},{2,18},{3,19},{4,20},{5,21},{6,22},{7,23},{8,9},{9,8... | collective-permute-start | bytes 786440 | tf_op jit(solution)/shard_map/ppermute | solution.py:296
  112.0 21.3 %collective-permute-start.22 = (bf16[1,512,256]{2,1,0:T(8,128)(2,1)}, bf16[1,512,256]{2,1,0:T(8,128)(2,1)S(1)}, u32[]{:S(2)}, u32[]{:S(2)}) collective-permute-start(bf16[1,512,256]{2,1,0:T(8,128)(2,1)} %get-tuple-element.27), channel_id=1, source_target_pairs={{0,2},{1,3},{2,4},{3,5},{4,6},{5,7},{6,0},{7,1},{8,10},{9,11},{10,... | collective-permute-start | bytes 786440 | tf_op jit(solution)/shard_map/ppermute | solution.py:296
  112.9 22.4 %collective-permute-start.23 = (bf16[1,512,256]{2,1,0:T(8,128)(2,1)}, bf16[1,512,256]{2,1,0:T(8,128)(2,1)S(1)}, u32[]{:S(2)}, u32[]{:S(2)}) collective-permute-start(bf16[1,512,256]{2,1,0:T(8,128)(2,1)} %get-tuple-element.26), channel_id=1, source_target_pairs={{0,6},{1,7},{2,0},{3,1},{4,2},{5,3},{6,4},{7,5},{8,14},{9,15},{10,... | collective-permute-start | bytes 786440 | tf_op jit(solution)/shard_map/ppermute | solution.py:296
